TPU v7x, 32 devices: a whole 2x2x4 slice. The times are simulated.
32 devices in a mesh: batch: 16 (over z, y, core), head: 2 (over x).
Axes of the slice: x: 2, y: 2, z: 4, core: 2. Of those that a mesh axis runs over, the one named last changes fastest.
Arguments:
- images: bfloat16 [32, 512, 1024], P('batch', 'head'), may hold values from -6 to 6
- timesteps: int32 [32], P('batch'), may hold values from 0 to 999
- classes: int32 [32], P('batch'), may hold values from 0 to 999
- live_count: int32 [16], P('batch'), may hold values from 1 to 2, as said below
- norm_gain: float32 [3, 512], P(None, 'head'), may hold values from 0.1 to 1.9
- norm_bias: float32 [3, 512], P(None, 'head'), may hold values from -3 to 3
- conv_weight: bfloat16 [2, 9, 512, 512], P(None, None, 'head'), may hold values from -0.09375 to 0.09375
- conv_bias: float32 [2, 512], P(None, 'head'), may hold values from -3 to 3
- emb_weight: bfloat16 [2, 512, 1024], P(None, 'head'), may hold values from -0.1875 to 0.1875
- emb_bias: float32 [2, 512], P(None, 'head'), may hold values from -2 to 2
- class_table: bfloat16 [1000, 1024], replicated, may hold values from -6 to 6
- qkv_weight: bfloat16 [3, 512, 512], P(None, 'head'), may hold values from -0.25 to 0.25
- proj_weight: bfloat16 [512, 512], P('head'), may hold values from -4 to 4
- proj_bias: float32 [512], P('head'), may hold values from -3 to 3
- cotangent: bfloat16 [32, 512, 1024], P('batch', 'head'), may hold values from -6 to 6
Outputs:
- block_out: bfloat16 [32, 512, 1024], P('batch', 'head')
- images_grad: float32 [32, 512, 1024], P('batch', 'head')
- norm_gain_grad: float32 [3, 512], P(None, 'head')
- norm_bias_grad: float32 [3, 512], P(None, 'head')
- conv_weight_grad: float32 [2, 9, 512, 512], P(None, None, 'head')
- conv_bias_grad: float32 [2, 512], P(None, 'head')
- emb_weight_grad: float32 [2, 512, 1024], P(None, 'head')
- emb_bias_grad: float32 [2, 512], P(None, 'head')
- class_table_grad: float32 [1000, 1024], replicated
- qkv_weight_grad: float32 [3, 512, 512], P(None, 'head')
- proj_weight_grad: float32 [512, 512], P('head')
- proj_bias_grad: float32 [512], P('head')
Inputs may be any that keep to these rules, and one draw needn't show every extreme that they name: Slots 0 to live_count - 1 of each index of batch hold images; the others are padding. One index holds 2.
All inputs are finite; a program needn't handle non-finite values.
Results may differ from a plain program's by a relative error of at most 0.02.
Values may be sent and summed in bfloat16 or wider, within the bound.
A program may use at most 192 MiB of HBM per device.

v0:
```python
import math

import jax
import jax.numpy as jnp
from jax import lax
from jax.sharding import PartitionSpec as P

C = 512
GROUPS = 32
HEADS = 8
SIDE = 32


EPS = 1e-05
HIGH = lax.Precision.HIGHEST
CONTRACT_FIRST = (((0,), (0,)), ((), ()))
CONTRACT_LAST = (((1,), (1,)), ((), ()))


def silu_slope(values):
    sigma = jax.nn.sigmoid(values)
    return sigma * (1.0 + values * (1.0 - sigma))


def moved(source, grid_side, row_step, col_step):
    grid = source.reshape(source.shape[0], grid_side, grid_side)
    padded = jnp.pad(grid, ((0, 0), (1, 1), (1, 1)))
    window = padded[
        :, 1 + row_step : 1 + row_step + grid_side, 1 + col_step : 1 + col_step + grid_side
    ]
    return window.reshape(source.shape)


def group_unit(source, groups):
    grouped = source.reshape(groups, -1)
    centre = grouped - jnp.mean(grouped, axis=1, keepdims=True)
    inverse = lax.rsqrt(jnp.mean(jnp.square(centre), axis=1, keepdims=True) + EPS)
    return ((centre * inverse).reshape(source.shape), inverse)


def group_back(grad_unit, unit_rows, inverse, groups):
    flat_grad = grad_unit.reshape(groups, -1)
    flat_unit = unit_rows.reshape(groups, -1)
    result = flat_grad - jnp.mean(flat_grad, axis=1, keepdims=True)
    result = (result - flat_unit * jnp.mean(flat_grad * flat_unit, axis=1, keepdims=True)) * inverse
    return result.reshape(grad_unit.shape)


def conv_apply(weight, source, grid_side):
    result = jnp.dot(
        weight[0], moved(source, grid_side, -1, -1), preferred_element_type=jnp.float32
    )
    for tap_index in range(1, 9):
        result = result + jnp.dot(
            weight[tap_index],
            moved(source, grid_side, tap_index // 3 - 1, tap_index % 3 - 1),
            preferred_element_type=jnp.float32,
        )
    return result


def conv_transpose(weight, grads, grid_side):
    result = lax.dot_general(
        weight[0], moved(grads, grid_side, 1, 1), CONTRACT_FIRST, preferred_element_type=jnp.float32
    )
    for tap_index in range(1, 9):
        result = result + lax.dot_general(
            weight[tap_index],
            moved(grads, grid_side, 1 - tap_index // 3, 1 - tap_index % 3),
            CONTRACT_FIRST,
            preferred_element_type=jnp.float32,
        )
    return result


def conv_weight_grads(grads, source, grid_side):
    return jnp.stack(
        [
            lax.dot_general(
                grads,
                moved(source, grid_side, tap_index // 3 - 1, tap_index % 3 - 1),
                CONTRACT_LAST,
                preferred_element_type=jnp.float32,
            )
            for tap_index in range(9)
        ]
    )


def features(timestep, emb_width):
    half_width = emb_width // 2
    freqs = jnp.exp(-math.log(10000.0) * jnp.arange(half_width, dtype=jnp.float32) / half_width)
    angles = timestep.astype(jnp.float32) * freqs
    return jnp.concatenate([jnp.cos(angles), jnp.sin(angles)])


def shards(
    images,
    timesteps,
    classes,
    live_count,
    norm_gain,
    norm_bias,
    conv_weight,
    conv_bias,
    emb_weight,
    emb_bias,
    class_table,
    qkv_weight,
    proj_weight,
    proj_bias,
    cotangent,
):
    slot_count, chan_dev, pixel_count = images.shape
    grid_side = SIDE
    groups = chan_dev // (C // GROUPS)
    head_size = C // HEADS
    heads_dev = chan_dev // head_size
    att_scale = head_size ** (-0.5)
    emb_dense = emb_weight.astype(jnp.float32)
    class_total, emb_width = class_table.shape

    def gather_channels(rows_low):
        return lax.all_gather(rows_low, "head", axis=0, tiled=True)

    def input_grad(which_conv, grad_rows):
        weight_cols = conv_weight[which_conv]
        return lax.psum_scatter(
            conv_transpose(weight_cols, grad_rows, grid_side).astype(jnp.bfloat16),
            "head",
            scatter_dimension=0,
            tiled=True,
        ).astype(jnp.float32)

    def per_slot(slot_index, carry):
        (
            outputs,
            grads_in,
            gain_acc,
            bias_acc,
            convw_acc,
            convb_acc,
            embw_acc,
            embb_acc,
            table_acc,
            qkv_acc,
            projw_acc,
            projb_acc,
        ) = carry
        picture = lax.dynamic_index_in_dim(images, slot_index, 0, keepdims=False).astype(
            jnp.float32
        )
        live_flag = (slot_index < live_count[0]).astype(jnp.float32)
        class_id = classes[slot_index]
        table_row = lax.dynamic_index_in_dim(class_table, class_id, 0, keepdims=False).astype(
            jnp.float32
        )
        pre_embed = features(timesteps[slot_index], emb_width) + table_row
        embed = jax.nn.silu(pre_embed)
        scale = jnp.dot(emb_dense[0], embed, precision=HIGH) + emb_bias[0]
        shift = jnp.dot(emb_dense[1], embed, precision=HIGH) + emb_bias[1]
        unit_zero, inverse_zero = group_unit(picture, groups)
        pre_first = unit_zero * norm_gain[0][:, None] + norm_bias[0][:, None]
        first_full = gather_channels(jax.nn.silu(pre_first).astype(jnp.bfloat16))
        hidden = conv_apply(conv_weight[0], first_full, grid_side) + conv_bias[0][:, None]
        unit_one, inverse_one = group_unit(hidden, groups)
        normed_one = unit_one * norm_gain[1][:, None] + norm_bias[1][:, None]
        pre_second = normed_one * (1.0 + scale[:, None]) + shift[:, None]
        second_full = gather_channels(jax.nn.silu(pre_second).astype(jnp.bfloat16))
        resid = picture + conv_apply(conv_weight[1], second_full, grid_side) + conv_bias[1][:, None]
        unit_two, inverse_two = group_unit(resid, groups)
        normed_full = gather_channels(
            (unit_two * norm_gain[2][:, None] + norm_bias[2][:, None]).astype(jnp.bfloat16)
        )
        query = (
            jnp.dot(qkv_weight[0], normed_full, preferred_element_type=jnp.float32)
            .astype(jnp.bfloat16)
            .reshape(heads_dev, head_size, pixel_count)
        )
        keys = (
            jnp.dot(qkv_weight[1], normed_full, preferred_element_type=jnp.float32)
            .astype(jnp.bfloat16)
            .reshape(heads_dev, head_size, pixel_count)
        )
        values = (
            jnp.dot(qkv_weight[2], normed_full, preferred_element_type=jnp.float32)
            .astype(jnp.bfloat16)
            .reshape(heads_dev, head_size, pixel_count)
        )
        scores = (
            jnp.einsum("hdi,hdj->hij", query, keys, preferred_element_type=jnp.float32) * att_scale
        )
        highest = jnp.max(scores, axis=2, keepdims=True)
        expo = jnp.exp(scores - highest)
        totals = jnp.sum(expo, axis=2, keepdims=True)
        log_total = highest + jnp.log(totals)
        weights = (expo / totals).astype(jnp.bfloat16)
        mixed = (
            jnp.einsum("hdj,hij->hdi", values, weights, preferred_element_type=jnp.float32)
            .astype(jnp.bfloat16)
            .reshape(chan_dev, pixel_count)
        )
        weight_cols = proj_weight
        proj_term = lax.psum_scatter(
            lax.dot_general(
                weight_cols, mixed, CONTRACT_FIRST, preferred_element_type=jnp.float32
            ).astype(jnp.bfloat16),
            "head",
            scatter_dimension=0,
            tiled=True,
        ).astype(jnp.float32)
        result = resid + proj_term + proj_bias[:, None]
        outputs = lax.dynamic_update_index_in_dim(
            outputs, (live_flag * result).astype(jnp.bfloat16), slot_index, 0
        )
        grad_low = lax.dynamic_index_in_dim(cotangent, slot_index, 0, keepdims=False)
        grad_out = live_flag * grad_low.astype(jnp.float32)
        grad_full = lax.all_gather(grad_low, "head", axis=0, tiled=True) * live_flag.astype(
            jnp.bfloat16
        )
        grad_mixed = jnp.dot(proj_weight, grad_full, preferred_element_type=jnp.float32).astype(
            jnp.bfloat16
        )
        projw_acc = projw_acc + lax.dot_general(
            mixed, grad_full, CONTRACT_LAST, preferred_element_type=jnp.float32
        )
        projb_acc = projb_acc + jnp.sum(grad_out, axis=1)
        again = (
            jnp.einsum("hdi,hdj->hij", query, keys, preferred_element_type=jnp.float32) * att_scale
        )
        probs = jnp.exp(again - log_total)
        grad_heads = grad_mixed.reshape(heads_dev, head_size, pixel_count)
        grad_probs = jnp.einsum(
            "hdi,hdj->hij", grad_heads, values, preferred_element_type=jnp.float32
        )
        grad_scores = (
            probs * (grad_probs - jnp.sum(grad_probs * probs, axis=2, keepdims=True))
        ).astype(jnp.bfloat16)
        grad_query = (
            jnp.einsum("hij,hdj->hdi", grad_scores, keys, preferred_element_type=jnp.float32)
            * att_scale
        ).astype(jnp.bfloat16)
        grad_keys = (
            jnp.einsum("hij,hdi->hdj", grad_scores, query, preferred_element_type=jnp.float32)
            * att_scale
        ).astype(jnp.bfloat16)
        grad_values = jnp.einsum(
            "hdi,hij->hdj", grad_heads, weights, preferred_element_type=jnp.float32
        ).astype(jnp.bfloat16)
        stacked = jnp.stack([grad_query, grad_keys, grad_values]).reshape(3, chan_dev, pixel_count)
        weight_cols = qkv_weight
        grad_normed = lax.psum_scatter(
            lax.dot_general(
                weight_cols,
                stacked,
                (((0, 1), (0, 1)), ((), ())),
                preferred_element_type=jnp.float32,
            ).astype(jnp.bfloat16),
            "head",
            scatter_dimension=0,
            tiled=True,
        ).astype(jnp.float32)
        qkv_acc = qkv_acc + lax.dot_general(
            stacked, normed_full, (((2,), (1,)), ((), ())), preferred_element_type=jnp.float32
        )
        grad_resid = grad_out + group_back(
            grad_normed * norm_gain[2][:, None], unit_two, inverse_two, groups
        )
        grad_branch = grad_resid.astype(jnp.bfloat16)
        grad_second = input_grad(1, grad_branch)
        grad_pre = grad_second * silu_slope(pre_second)
        scale_grad = jnp.sum(grad_pre * normed_one, axis=1)
        shift_grad = jnp.sum(grad_pre, axis=1)
        grad_normed_one = grad_pre * (1.0 + scale[:, None])
        grad_hidden = group_back(
            grad_normed_one * norm_gain[1][:, None], unit_one, inverse_one, groups
        ).astype(jnp.bfloat16)
        grad_first = input_grad(0, grad_hidden)
        grad_pre_first = grad_first * silu_slope(pre_first)
        picture_grad = grad_resid + group_back(
            grad_pre_first * norm_gain[0][:, None], unit_zero, inverse_zero, groups
        )
        grads_in = lax.dynamic_update_index_in_dim(grads_in, picture_grad, slot_index, 0)
        gain_acc = gain_acc + jnp.stack(
            [
                jnp.sum(grad_pre_first * unit_zero, axis=1),
                jnp.sum(grad_normed_one * unit_one, axis=1),
                jnp.sum(grad_normed * unit_two, axis=1),
            ]
        )
        bias_acc = bias_acc + jnp.stack(
            [
                jnp.sum(grad_pre_first, axis=1),
                jnp.sum(grad_normed_one, axis=1),
                jnp.sum(grad_normed, axis=1),
            ]
        )
        convw_acc = convw_acc + jnp.stack(
            [
                conv_weight_grads(grad_hidden, first_full, grid_side),
                conv_weight_grads(grad_branch, second_full, grid_side),
            ]
        )
        convb_acc = convb_acc + jnp.stack(
            [
                jnp.sum(grad_hidden.astype(jnp.float32), axis=1),
                jnp.sum(grad_branch.astype(jnp.float32), axis=1),
            ]
        )
        embw_acc = embw_acc + jnp.stack(
            [scale_grad[:, None] * embed[None, :], shift_grad[:, None] * embed[None, :]]
        )
        embb_acc = embb_acc + jnp.stack([scale_grad, shift_grad])
        grad_embed = jnp.dot(scale_grad, emb_dense[0], precision=HIGH) + jnp.dot(
            shift_grad, emb_dense[1], precision=HIGH
        )
        class_row = grad_embed * silu_slope(pre_embed)
        old_row = lax.dynamic_index_in_dim(table_acc, class_id, 0, keepdims=True)
        table_acc = lax.dynamic_update_index_in_dim(
            table_acc, old_row + class_row[None, :], class_id, 0
        )
        return (
            outputs,
            grads_in,
            gain_acc,
            bias_acc,
            convw_acc,
            convb_acc,
            embw_acc,
            embb_acc,
            table_acc,
            qkv_acc,
            projw_acc,
            projb_acc,
        )

    table_start = jnp.zeros(class_table.shape, jnp.float32)
    initial = (
        jnp.zeros(images.shape, jnp.bfloat16),
        jnp.zeros(images.shape, jnp.float32),
        jnp.zeros(norm_gain.shape, jnp.float32),
        jnp.zeros(norm_bias.shape, jnp.float32),
        jnp.zeros(conv_weight.shape, jnp.float32),
        jnp.zeros(conv_bias.shape, jnp.float32),
        jnp.zeros(emb_weight.shape, jnp.float32),
        jnp.zeros(emb_bias.shape, jnp.float32),
        table_start,
        jnp.zeros(qkv_weight.shape, jnp.float32),
        jnp.zeros(proj_weight.shape, jnp.float32),
        jnp.zeros(proj_bias.shape, jnp.float32),
    )
    final = lax.fori_loop(0, slot_count, per_slot, initial)
    (
        outputs,
        grads_in,
        gain_acc,
        bias_acc,
        convw_acc,
        convb_acc,
        embw_acc,
        embb_acc,
        table_acc,
        qkv_acc,
        projw_acc,
        projb_acc,
    ) = final
    table_total = lax.psum(table_acc, ("batch", "head"))
    summed = (
        lax.psum(gain_acc.astype(jnp.bfloat16), "batch").astype(jnp.float32),
        lax.psum(bias_acc.astype(jnp.bfloat16), "batch").astype(jnp.float32),
        lax.psum(convw_acc.astype(jnp.bfloat16), "batch").astype(jnp.float32),
        lax.psum(convb_acc.astype(jnp.bfloat16), "batch").astype(jnp.float32),
        lax.psum(embw_acc.astype(jnp.bfloat16), "batch").astype(jnp.float32),
        lax.psum(embb_acc.astype(jnp.bfloat16), "batch").astype(jnp.float32),
        lax.psum(qkv_acc.astype(jnp.bfloat16), "batch").astype(jnp.float32),
        lax.psum(projw_acc.astype(jnp.bfloat16), "batch").astype(jnp.float32),
        lax.psum(projb_acc.astype(jnp.bfloat16), "batch").astype(jnp.float32),
    )
    return (
        outputs,
        grads_in,
        summed[0],
        summed[1],
        summed[2],
        summed[3],
        summed[4],
        summed[5],
        table_total,
        summed[6],
        summed[7],
        summed[8],
    )


def solution(mesh):
    in_specs = (
        P("batch", "head", None),
        P("batch"),
        P("batch"),
        P("batch"),
        P(None, "head"),
        P(None, "head"),
        P(None, None, "head", None),
        P(None, "head"),
        P(None, "head", None),
        P(None, "head"),
        P(),
        P(None, "head", None),
        P("head", None),
        P("head"),
        P("batch", "head", None),
    )
    out_specs = (
        P("batch", "head", None),
        P("batch", "head", None),
        P(None, "head"),
        P(None, "head"),
        P(None, None, "head", None),
        P(None, "head"),
        P(None, "head", None),
        P(None, "head"),
        P(),
        P(None, "head", None),
        P("head", None),
        P("head"),
    )
    return jax.shard_map(shards, mesh=mesh, in_specs=in_specs, out_specs=out_specs, check_vma=False)
```

profile of v0, /device:TPU:0, one launch (start us, length us, event | category | flops | bytes accessed | tf_op | source)
XLA Modules:
  0.0 1001.5 jit_solution(13179502503955031552)
XLA Ops:
  12.2 671.7 %while.38 = (s32[]{:T(128)}, bf16[2,256,1024]{2,1,0:T(8,128)(2,1)}, f32[2,256,1024]{2,1,0:T(8,128)}, f32[3,256]{1,0:T(4,128)S(1)}, f32[3,256]{1,0:T(4,128)S(1)},...) while((s32[]{:T(128)}, bf16[2,256,1024]{2,1,0:T(8,128)(2,1)}, ...), condition=%wide.region_43.44_spmd.clone, body=%wide.region_0.43_spmd.clone.sunk | while | flops 21093961728 | bytes 815259776 | solution.py:352
  24.5 16.2 %all-gather.9.cloned.1.call-done = bf16[512,1024]{0,1:T(8,128)(2,1)} async-done(((bf16[256,1024]{0,1:T(8,128)(2,1)}), bf16[512,1024]{0,1:T(8,128)(2,1)}) %all-gather.9.cloned.1.call-update) | async-done | bytes 1048592 | tf_op jit(solution)/shard_map/while/body/eval_jaxpr/all_gather | solution.py:124
  40.7 6.7 pad_slice_fusion.36
  58.1 18.5 %all-gather.13.cloned.1.call-done = bf16[512,1024]{0,1:T(8,128)(2,1)} async-done(((bf16[256,1024]{0,1:T(8,128)(2,1)}), bf16[512,1024]{0,1:T(8,128)(2,1)}) %all-gather.13.cloned.1.call-update) | async-done | bytes 1048592 | tf_op jit(solution)/shard_map/while/body/eval_jaxpr/all_gather | solution.py:124
  76.6 6.6 pad_slice_fusion.37
  102.3 19.8 %all-gather.15.cloned.1.call-done = bf16[512,1024]{0,1:T(8,128)(2,1)} async-done(((bf16[256,1024]{0,1:T(8,128)(2,1)}), bf16[512,1024]{0,1:T(8,128)(2,1)}) %all-gather.15.cloned.1.call-update) | async-done | bytes 1048592 | tf_op jit(solution)/shard_map/while/body/eval_jaxpr/all_gather | solution.py:124
  125.6 8.1 multiply_reduce_fusion.15
  133.8 8.6 fusion.653
  144.6 14.3 %multiply_reduce_fusion.16 = (f32[4,1024]{1,0:T(4,128)S(1)}, f32[4,1024,1024]{1,2,0:T(8,128)}) fusion(f32[4,1024,1024]{1,2,0:T(8,128)} %get-tuple-element.1274, f32[4,1024]{1,0:T(4,128)S(1)} %log_add_fusion.2, bf16[4,64,1024]{2,1,0:T(8,128)(2,1)} %bitcast.1033, bf16[4,64,1024]{2,1,0:T(8,128)(2,1)} %bitcast.1031), kind=kOutput, calls=%fused_computation.1.clone.1 | convolution fusion | flops 553644032 | bytes 34635776 | tf_op jit(solution)/shard_map/while/body/eval_jaxpr/hdi,hdj->hij/dot_general | solution.py:233
  161.4 14.4 %multiply_convert_fusion.6 = (bf16[4,1024,1024]{1,2,0:T(8,128)(2,1)}, bf16[4,1024,1024]{1,2,0:T(8,128)(2,1)}) fusion(f32[4,1024,1024]{1,2,0:T(8,128)} %get-tuple-element.1276, f32[4,1024,1024]{1,2,0:T(8,128)S(1)} %bitcast.985, f32[4,1024]{1,0:T(4,128)S(1)} %get-tuple-element.1277, f32[4,1024]{1,0:T(4,128)S(1)} %log_add_fusion.2, ...), kind=kLoop, calls=%fused_computation.clone.1 | loop fusion | flops 33554432 | bytes 50397184 | tf_op jit(solution)/shard_map/while/body/eval_jaxpr/convert_element_type | solution.py:238
  189.2 6.9 convolution_convert_fusion.17
  202.3 20.0 %reduce-scatter.5.cloned.1.call-done = bf16[256,1024]{0,1:T(8,128)(2,1)} async-done(((bf16[512,1024]{0,1:T(8,128)(2,1)}), bf16[256,1024]{0,1:T(8,128)(2,1)}) %reduce-scatter.5.cloned.1.call-update) | async-done | bytes 524304 | tf_op jit(solution)/shard_map/while/body/eval_jaxpr/reduce_scatter | solution.py:252
  241.1 20.4 %reduce-scatter.7.cloned.1.call-done = bf16[256,1024]{0,1:T(8,128)(2,1)} async-done(((bf16[512,1024]{0,1:T(8,128)(2,1)}), bf16[256,1024]{0,1:T(8,128)(2,1)}) %reduce-scatter.7.cloned.1.call-update) | async-done | bytes 524304 | tf_op jit(solution)/shard_map/while/body/eval_jaxpr/reduce_scatter | solution.py:128
  321.6 10.7 %maximum_add_fusion.13 = f32[2,9,256,512]{3,2,1,0:T(8,128)} fusion(f32[1,9,256,512]{3,2,1,0:T(8,128)} %bitcast.992, f32[1,9,256,512]{3,2,1,0:T(8,128)} %bitcast.972, f32[2,9,256,512]{3,2,1,0:T(8,128)} %get-tuple-element.1364, pred[]{:T(512)S(6)} %compare.7), kind=kLoop, calls=%fused_computation.7.clone.1 | loop fusion | flops 7077888 | bytes 28311552 | tf_op jit(solution)/shard_map/while/body/eval_jaxpr/add | solution.py:298
  358.3 13.5 %all-gather.9.cloned.1.call-done = bf16[512,1024]{0,1:T(8,128)(2,1)} async-done(((bf16[256,1024]{0,1:T(8,128)(2,1)}), bf16[512,1024]{0,1:T(8,128)(2,1)}) %all-gather.9.cloned.1.call-update) | async-done | bytes 1048592 | tf_op jit(solution)/shard_map/while/body/eval_jaxpr/all_gather | solution.py:124
  371.9 6.7 pad_slice_fusion.36
  389.0 18.8 %all-gather.13.cloned.1.call-done = bf16[512,1024]{0,1:T(8,128)(2,1)} async-done(((bf16[256,1024]{0,1:T(8,128)(2,1)}), bf16[512,1024]{0,1:T(8,128)(2,1)}) %all-gather.13.cloned.1.call-update) | async-done | bytes 1048592 | tf_op jit(solution)/shard_map/while/body/eval_jaxpr/all_gather | solution.py:124
  407.8 6.6 pad_slice_fusion.37
  433.5 19.8 %all-gather.15.cloned.1.call-done = bf16[512,1024]{0,1:T(8,128)(2,1)} async-done(((bf16[256,1024]{0,1:T(8,128)(2,1)}), bf16[512,1024]{0,1:T(8,128)(2,1)}) %all-gather.15.cloned.1.call-update) | async-done | bytes 1048592 | tf_op jit(solution)/shard_map/while/body/eval_jaxpr/all_gather | solution.py:124
  456.8 8.1 multiply_reduce_fusion.15
  465.0 8.6 fusion.653
  475.8 14.3 %multiply_reduce_fusion.16 = (f32[4,1024]{1,0:T(4,128)S(1)}, f32[4,1024,1024]{1,2,0:T(8,128)}) fusion(f32[4,1024,1024]{1,2,0:T(8,128)} %get-tuple-element.1274, f32[4,1024]{1,0:T(4,128)S(1)} %log_add_fusion.2, bf16[4,64,1024]{2,1,0:T(8,128)(2,1)} %bitcast.1033, bf16[4,64,1024]{2,1,0:T(8,128)(2,1)} %bitcast.1031), kind=kOutput, calls=%fused_computation.1.clone.1 | convolution fusion | flops 553644032 | bytes 34635776 | tf_op jit(solution)/shard_map/while/body/eval_jaxpr/hdi,hdj->hij/dot_general | solution.py:233
  492.6 14.4 %multiply_convert_fusion.6 = (bf16[4,1024,1024]{1,2,0:T(8,128)(2,1)}, bf16[4,1024,1024]{1,2,0:T(8,128)(2,1)}) fusion(f32[4,1024,1024]{1,2,0:T(8,128)} %get-tuple-element.1276, f32[4,1024,1024]{1,2,0:T(8,128)S(1)} %bitcast.985, f32[4,1024]{1,0:T(4,128)S(1)} %get-tuple-element.1277, f32[4,1024]{1,0:T(4,128)S(1)} %log_add_fusion.2, ...), kind=kLoop, calls=%fused_computation.clone.1 | loop fusion | flops 33554432 | bytes 50397184 | tf_op jit(solution)/shard_map/while/body/eval_jaxpr/convert_element_type | solution.py:238
  520.4 6.9 convolution_convert_fusion.17
  533.5 20.0 %reduce-scatter.5.cloned.1.call-done = bf16[256,1024]{0,1:T(8,128)(2,1)} async-done(((bf16[512,1024]{0,1:T(8,128)(2,1)}), bf16[256,1024]{0,1:T(8,128)(2,1)}) %reduce-scatter.5.cloned.1.call-update) | async-done | bytes 524304 | tf_op jit(solution)/shard_map/while/body/eval_jaxpr/reduce_scatter | solution.py:252
  572.2 20.4 %reduce-scatter.7.cloned.1.call-done = bf16[256,1024]{0,1:T(8,128)(2,1)} async-done(((bf16[512,1024]{0,1:T(8,128)(2,1)}), bf16[256,1024]{0,1:T(8,128)(2,1)}) %reduce-scatter.7.cloned.1.call-update) | async-done | bytes 524304 | tf_op jit(solution)/shard_map/while/body/eval_jaxpr/reduce_scatter | solution.py:128
  654.0 13.4 %maximum_add_fusion.13 = f32[2,9,256,512]{3,2,1,0:T(8,128)} fusion(f32[1,9,256,512]{3,2,1,0:T(8,128)} %bitcast.992, f32[1,9,256,512]{3,2,1,0:T(8,128)} %bitcast.972, f32[2,9,256,512]{3,2,1,0:T(8,128)} %get-tuple-element.1364, pred[]{:T(512)S(6)} %compare.7), kind=kLoop, calls=%fused_computation.7.clone.1 | loop fusion | flops 7077888 | bytes 28311552 | tf_op jit(solution)/shard_map/while/body/eval_jaxpr/add | solution.py:298
  684.0 6.7 convert_element_type.512
  694.2 36.0 %all-reduce.4 = (bf16[3,256]{1,0:T(4,128)(2,1)S(1)}, bf16[3,256]{1,0:T(4,128)(2,1)S(1)}, bf16[2,256]{1,0:T(2,128)(2,1)S(1)}, bf16[2,256]{1,0:T(2,128)(2,1)S(1)}, bf16[256]{0:T(256)(128)(2,1)S(1)}) all-reduce(bf16[3,256]{1,0:T(4,128)(2,1)S(1)} %convert_element_type.508, ...), channel_id=1, replica_groups=mesh['batch'=16,'head'=2] {'batch'}, use_global_device_ids=true, to_apply=%region_44.45 | all-reduce | flops 2816 | bytes 11264 | tf_op jit(solution)/shard_map/psum | solution.py:369
  733.1 109.6 %all-reduce.11.cloned.1.call-done = (bf16[2,9,256,512]{3,2,1,0:T(8,128)(2,1)}, bf16[2,256,1024]{2,1,0:T(8,128)(2,1)}, bf16[3,256,512]{2,1,0:T(8,128)(2,1)}, bf16[256,512]{1,0:T(8,128)(2,1)}) async-done(((bf16[2,9,256,512]{3,2,1,0:T(8,128)(2,1)}, bf16[2,256,1024]{2,1,0:T(8,128)(2,1)}, bf16[3,256,512]{2,1,0:T(8,128)(2,1)}, bf16[256,512]{1,0:T(8,128)(2,1)}), (bf16[2,9,256,512]{3,2,1,0:T(8,128)(2,1)}, ...) | async-done | bytes 6815760 | tf_op jit(solution)/shard_map/psum | solution.py:371
  842.7 7.5 convert_element_type.513
  854.0 135.4 %all-reduce.9.cloned.1.call-done = f32[1000,1024]{1,0:T(8,128)} async-done(((f32[1000,1024]{1,0:T(8,128)}), f32[1000,1024]{1,0:T(8,128)}) %all-reduce.9.cloned.1.call-update) | async-done | bytes 4096016 | tf_op jit(solution)/shard_map/psum | solution.py:367
  (706 shorter events, 335.2 us)
Async XLA Ops:
  12.5 28.2 %all-gather.9.cloned.1.call-start = ((), (), s32[]{:S(2)}) async-start(), calls=%async_computation.6 | async-start | bytes 1572864 | tf_op jit(solution)/shard_map/while/body/eval_jaxpr/all_gather | solution.py:124
  16.6 60.0 %all-gather.13.cloned.1.call-start = ((), (), s32[]{:S(2)}) async-start(), calls=%async_computation.8 | async-start | bytes 1572864 | tf_op jit(solution)/shard_map/while/body/eval_jaxpr/all_gather | solution.py:124
  22.3 25.2 %slice-start.4 = ((s8[4718592]{0:T(1024)(128)(4,1)}), s8[524288]{0:T(1024)(128)(4,1)S(1)}, s32[]{:S(2)}) async-start(s8[4718592]{0:T(1024)(128)(4,1)} %bitcast.986), calls=%async_computation.18 | async-start | bytes 1048576 | tf_op jit(solution)/shard_map/while
  55.2 44.6 %all-gather.11.cloned.1.call-start = ((), (), s32[]{:S(2)}) async-start(), calls=%async_computation.7 | async-start | bytes 1572864 | tf_op jit(solution)/shard_map/while/body/eval_jaxpr/all_gather | solution.py:218
  57.4 64.8 %all-gather.15.cloned.1.call-start = ((), (), s32[]{:S(2)}) async-start(), calls=%async_computation.9 | async-start | bytes 1572864 | tf_op jit(solution)/shard_map/while/body/eval_jaxpr/all_gather | solution.py:124
  98.9 123.4 %reduce-scatter.5.cloned.1.call-start = ((), (), s32[]{:S(2)}) async-start(), calls=%async_computation.10 | async-start | bytes 1572864 | tf_op jit(solution)/shard_map/while/body/eval_jaxpr/reduce_scatter | solution.py:252
  144.6 14.3 %slice-start = ((s8[16777216]{0:T(1024)(128)(4,1)}), s8[4194304]{0:T(1024)(128)(4,1)S(1)}, s32[]{:S(2)}) async-start(s8[16777216]{0:T(1024)(128)(4,1)} %bitcast.984), calls=%async_computation.14 | async-start | bytes 8388608 | tf_op jit(solution)/shard_map/while
  144.6 14.3 %slice-start.1 = ((s8[16777216]{0:T(1024)(128)(4,1)}), s8[4194304]{0:T(1024)(128)(4,1)S(1)}, s32[]{:S(2)}) async-start(s8[16777216]{0:T(1024)(128)(4,1)} %bitcast.984), calls=%async_computation.15 | async-start | bytes 8388608 | tf_op jit(solution)/shard_map/while
  144.6 15.5 %slice-start.2 = ((s8[16777216]{0:T(1024)(128)(4,1)}), s8[4194304]{0:T(1024)(128)(4,1)S(1)}, s32[]{:S(2)}) async-start(s8[16777216]{0:T(1024)(128)(4,1)} %bitcast.984), calls=%async_computation.16 | async-start | bytes 8388608 | tf_op jit(solution)/shard_map/while
  144.6 16.7 %slice-start.3 = ((s8[16777216]{0:T(1024)(128)(4,1)}), s8[4194304]{0:T(1024)(128)(4,1)S(1)}, s32[]{:S(2)}) async-start(s8[16777216]{0:T(1024)(128)(4,1)} %bitcast.984), calls=%async_computation.17 | async-start | bytes 8388608 | tf_op jit(solution)/shard_map/while
  198.2 26.3 %copy-start.1 = (bf16[1,256,1024]{1,2,0:T(8,128)(2,1)S(1)}, bf16[1,256,1024]{1,2,0:T(8,128)(2,1)}, u32[]{:S(2)}) copy-start(bf16[1,256,1024]{1,2,0:T(8,128)(2,1)} %copy.74) | copy-start | bytes 1572868 | tf_op jit(solution)/shard_map/while
  201.9 59.6 %reduce-scatter.7.cloned.1.call-start = ((), (), s32[]{:S(2)}) async-start(), calls=%async_computation.11 | async-start | bytes 1572864 | tf_op jit(solution)/shard_map/while/body/eval_jaxpr/reduce_scatter | solution.py:128
  241.0 91.3 %reduce-scatter.9.cloned.1.call-start = ((), (), s32[]{:S(2)}) async-start(), calls=%async_computation.12 | async-start | bytes 1572864 | tf_op jit(solution)/shard_map/while/body/eval_jaxpr/reduce_scatter | solution.py:128
  281.7 54.1 %reduce-scatter.11.cloned.1.call-start = ((), (), s32[]{:S(2)}) async-start(), calls=%async_computation.13 | async-start | bytes 1572864 | tf_op jit(solution)/shard_map/while/body/eval_jaxpr/reduce_scatter | solution.py:204
  346.2 25.6 %all-gather.9.cloned.1.call-start = ((), (), s32[]{:S(2)}) async-start(), calls=%async_computation.6 | async-start | bytes 1572864 | tf_op jit(solution)/shard_map/while/body/eval_jaxpr/all_gather | solution.py:124
  350.3 57.5 %all-gather.13.cloned.1.call-start = ((), (), s32[]{:S(2)}) async-start(), calls=%async_computation.8 | async-start | bytes 1572864 | tf_op jit(solution)/shard_map/while/body/eval_jaxpr/all_gather | solution.py:124
  356.0 22.6 %slice-start.4 = ((s8[4718592]{0:T(1024)(128)(4,1)}), s8[524288]{0:T(1024)(128)(4,1)S(1)}, s32[]{:S(2)}) async-start(s8[4718592]{0:T(1024)(128)(4,1)} %bitcast.986), calls=%async_computation.18 | async-start | bytes 1048576 | tf_op jit(solution)/shard_map/while
  386.3 44.7 %all-gather.11.cloned.1.call-start = ((), (), s32[]{:S(2)}) async-start(), calls=%async_computation.7 | async-start | bytes 1572864 | tf_op jit(solution)/shard_map/while/body/eval_jaxpr/all_gather | solution.py:218
  388.5 64.8 %all-gather.15.cloned.1.call-start = ((), (), s32[]{:S(2)}) async-start(), calls=%async_computation.9 | async-start | bytes 1572864 | tf_op jit(solution)/shard_map/while/body/eval_jaxpr/all_gather | solution.py:124
  430.1 123.4 %reduce-scatter.5.cloned.1.call-start = ((), (), s32[]{:S(2)}) async-start(), calls=%async_computation.10 | async-start | bytes 1572864 | tf_op jit(solution)/shard_map/while/body/eval_jaxpr/reduce_scatter | solution.py:252
  475.8 14.3 %slice-start = ((s8[16777216]{0:T(1024)(128)(4,1)}), s8[4194304]{0:T(1024)(128)(4,1)S(1)}, s32[]{:S(2)}) async-start(s8[16777216]{0:T(1024)(128)(4,1)} %bitcast.984), calls=%async_computation.14 | async-start | bytes 8388608 | tf_op jit(solution)/shard_map/while
  475.8 14.3 %slice-start.1 = ((s8[16777216]{0:T(1024)(128)(4,1)}), s8[4194304]{0:T(1024)(128)(4,1)S(1)}, s32[]{:S(2)}) async-start(s8[16777216]{0:T(1024)(128)(4,1)} %bitcast.984), calls=%async_computation.15 | async-start | bytes 8388608 | tf_op jit(solution)/shard_map/while
  475.8 15.5 %slice-start.2 = ((s8[16777216]{0:T(1024)(128)(4,1)}), s8[4194304]{0:T(1024)(128)(4,1)S(1)}, s32[]{:S(2)}) async-start(s8[16777216]{0:T(1024)(128)(4,1)} %bitcast.984), calls=%async_computation.16 | async-start | bytes 8388608 | tf_op jit(solution)/shard_map/while
  475.8 16.7 %slice-start.3 = ((s8[16777216]{0:T(1024)(128)(4,1)}), s8[4194304]{0:T(1024)(128)(4,1)S(1)}, s32[]{:S(2)}) async-start(s8[16777216]{0:T(1024)(128)(4,1)} %bitcast.984), calls=%async_computation.17 | async-start | bytes 8388608 | tf_op jit(solution)/shard_map/while
  529.4 26.3 %copy-start.1 = (bf16[1,256,1024]{1,2,0:T(8,128)(2,1)S(1)}, bf16[1,256,1024]{1,2,0:T(8,128)(2,1)}, u32[]{:S(2)}) copy-start(bf16[1,256,1024]{1,2,0:T(8,128)(2,1)} %copy.74) | copy-start | bytes 1572868 | tf_op jit(solution)/shard_map/while
  533.1 59.6 %reduce-scatter.7.cloned.1.call-start = ((), (), s32[]{:S(2)}) async-start(), calls=%async_computation.11 | async-start | bytes 1572864 | tf_op jit(solution)/shard_map/while/body/eval_jaxpr/reduce_scatter | solution.py:128
  572.2 95.2 %reduce-scatter.9.cloned.1.call-start = ((), (), s32[]{:S(2)}) async-start(), calls=%async_computation.12 | async-start | bytes 1572864 | tf_op jit(solution)/shard_map/while/body/eval_jaxpr/reduce_scatter | solution.py:128
  612.9 58.0 %reduce-scatter.11.cloned.1.call-start = ((), (), s32[]{:S(2)}) async-start(), calls=%async_computation.13 | async-start | bytes 1572864 | tf_op jit(solution)/shard_map/while/body/eval_jaxpr/reduce_scatter | solution.py:204
  654.0 16.9 %copy-start.4 = (bf16[256,1024]{0,1:T(8,128)(2,1)S(1)}, bf16[256,1024]{0,1:T(8,128)(2,1)}, u32[]{:S(2)}) copy-start(bf16[256,1024]{0,1:T(8,128)(2,1)} %reduce-scatter.5.cloned.1.call-done) | copy-start | bytes 1572868 | tf_op jit(solution)/shard_map/while
  654.0 16.9 %copy-start.61 = (f32[256]{0:T(256)S(1)}, f32[256]{0:T(256)}, u32[]{:S(2)}) copy-start(f32[256]{0:T(256)} %get-tuple-element.1417) | copy-start | bytes 3076 | tf_op jit(solution)/shard_map/while
  683.9 158.8 %all-reduce.11.cloned.1.call-start = ((), (), s32[]{:S(2)}) async-start(), calls=%async_computation.5 | async-start | bytes 13631488 | tf_op jit(solution)/shard_map/psum | solution.py:371
  693.5 295.9 %all-reduce.9.cloned.1.call-start = ((), (), s32[]{:S(2)}) async-start(), calls=%async_computation.4 | async-start | bytes 8192000 | tf_op jit(solution)/shard_map/psum | solution.py:367
  (124 other events, 613.1 us)
Sparse Core Ops, SparseCore 0:
  16.7 23.9 all-gather.8
  55.3 21.2 all-gather.12
  78.2 21.2 all-gather.10
  100.9 21.2 all-gather.14
  202.0 20.3 reduce-scatter.4
  241.1 20.3 reduce-scatter.6
  281.8 20.3 reduce-scatter.8
  304.5 20.3 reduce-scatter.10
  350.4 21.3 all-gather.8
  386.4 21.3 all-gather.12
  409.4 21.2 all-gather.10
  432.1 21.2 all-gather.14
  533.2 20.3 reduce-scatter.4
  572.3 20.3 reduce-scatter.6
  613.1 20.3 reduce-scatter.8
  635.6 20.3 reduce-scatter.10
Sparse Core Ops, SparseCore 1:
  693.6 149.0 all-reduce.10
  848.6 140.7 all-reduce.8
where the time goes:
time: 1010 us; the launch traced here: 1000 us
  waiting for transfers between devices  433 us (43%)
  matrix products  263 us (26%)
  other arithmetic  149 us (15%)
  local copies, waits for them, and re-layouts  88.6 us (9%)
  blocking collectives  36 us (4%)
  between operations  15.7 us (2%)
  loops' own time  12.6 us (1%)
    psum x1, waiting for transfers between devices, shards(): table_total = lax.psum(table_acc, ('batch', 'head'))  135 us
    psum x1, waiting for transfers between devices, shards(): lax.psum(convw_acc.astype(jnp.bfloat16), 'batch').astype(jnp.float32)  110 us
    all_gather x6, waiting for transfers between devices, gather_channels(): return lax.all_gather(rows_low, 'head', axis=0, tiled=True)  107 us
    dot_general x32, matrix products, conv_transpose(): lax.dot_general(weight[tap_index], moved(grads, grid_side, 1 - tap_index...  51.1 us
    reduce_scatter x4, waiting for transfers between devices, input_grad(): lax.psum_scatter(conv_transpose(weight_cols, grad_rows, grid_side).astype...  40.8 us
    reduce_scatter x2, waiting for transfers between devices, per_slot(): lax.psum_scatter(lax.dot_general(weight_cols, stacked, (((0, 1), (0, 1)),...  40 us
    psum x1, blocking collectives, shards(): lax.psum(gain_acc.astype(jnp.bfloat16), 'batch').astype(jnp.float32)  36 us
    dot_general x36, matrix products, conv_weight_grads(): lax.dot_general(grads, moved(source, grid_side, tap_index // 3 - 1, tap_i...  33.4 us
  transfers between devices with their start and end apart: 18, of which 12 were waited for; matrix products, arithmetic and copies ran while one was open for 19% of the time, Pallas kernels for 0%

commit v1 on v0

--- a/solution.py
+++ b/solution.py
@@ -1,8 +1,11 @@
+import functools
 import math
 
 import jax
 import jax.numpy as jnp
 from jax import lax
+from jax.experimental import pallas as pl
+from jax.experimental.pallas import tpu as pltpu
 from jax.sharding import PartitionSpec as P
 
 C = 512
@@ -392,6 +395,518 @@
     )
 
 
+PIX = 1024
+BF = jnp.bfloat16
+F32 = jnp.float32
+NN = (((1,), (0,)), ((), ()))
+TN = (((0,), (0,)), ((), ()))
+NT = (((1,), (1,)), ((), ()))
+VMEM = pl.BlockSpec(memory_space=pltpu.VMEM)
+SMEM = pl.BlockSpec(memory_space=pltpu.SMEM)
+
+GAIN, BIAS, CONVB, PROJB, SCALE, SHIFT = 0, 3, 6, 8, 9, 10
+
+
+def mm(left, right, dims=NN):
+    return lax.dot_general(left, right, dims, preferred_element_type=F32)
+
+
+def kernel_call(kernel, outs, scratch, flops, scalars, *args):
+    moved_bytes = sum(a.size * a.dtype.itemsize for a in args)
+    moved_bytes += sum(math.prod(o.shape) * o.dtype.itemsize for o in outs)
+    return pl.pallas_call(
+        kernel,
+        out_shape=outs,
+        in_specs=[SMEM] + [VMEM] * len(args),
+        out_specs=[VMEM] * len(outs),
+        scratch_shapes=scratch,
+        cost_estimate=pl.CostEstimate(flops=flops, bytes_accessed=moved_bytes, transcendentals=0),
+        compiler_params=pltpu.CompilerParams(vmem_limit_bytes=56 * 2**20),
+    )(scalars, *args)
+
+
+def out(shape, dtype):
+    return jax.ShapeDtypeStruct(shape, dtype)
+
+
+def rows(start, count):
+    return pl.ds(pl.multiple_of(start, count), count)
+
+
+def edge_masks(sign):
+    pixel = lax.broadcasted_iota(jnp.int32, (1, PIX), 1)
+    col, row = pixel % SIDE, pixel // SIDE
+    table = {}
+    for step in (-1, 1):
+        moved_step = sign * step
+        table["col", step] = ((col + moved_step >= 0) & (col + moved_step < SIDE)).astype(F32)
+        table["row", step] = ((row + moved_step >= 0) & (row + moved_step < SIDE)).astype(F32)
+    return table
+
+
+def put_taps(dest, masks, values, first_row, depth, base, sign):
+    count = values.shape[0]
+    for col_step in (-1, 0, 1):
+        across = values
+        if col_step:
+            across = pltpu.roll(values, (-sign * col_step) % PIX, 1) * masks["col", col_step]
+        for row_step in (-1, 0, 1):
+            copy = across
+            if row_step:
+                copy = pltpu.roll(across, (-sign * row_step * SIDE) % PIX, 1) * masks["row", row_step]
+            tap = 3 * (row_step + 1) + col_step + 1
+            dest[rows(tap * depth + first_row, count), base : base + PIX] = copy.astype(BF)
+
+
+def taps_of(dest, masks, source, offset, depth, base, sign):
+    def step(index, carry):
+        piece = source[rows(index * 16, 16), :].astype(F32)
+        put_taps(dest, masks, piece, offset + index * 16, depth, base, sign)
+        return carry
+
+    lax.fori_loop(0, source.shape[0] // 16, step, 0, unroll=2)
+
+
+def place_conv(full, index, own, part, peer):
+    half, core = index[0], index[1]
+    full[:, rows(half * 256, 256), :] = own[...]
+    full[:, rows((1 - half) * 256 + core * 128, 128), :] = part[...]
+    full[:, rows((1 - half) * 256 + (1 - core) * 128, 128), :] = peer[...]
+
+
+def conv_dots(dest, full, col, dims, finish):
+    for column in range(0, PIX, 512):
+        total = None
+        for tap in range(9):
+            term = mm(full[tap], col[tap * 512 : (tap + 1) * 512, column : column + 512], dims)
+            total = term if total is None else total + term
+        dest[:, column : column + 512] = finish(total, column)
+
+
+def group_stats(block):
+    centre = jnp.mean(block, keepdims=True)
+    moved_block = block - centre
+    inverse = lax.rsqrt(jnp.mean(jnp.square(moved_block), keepdims=True) + EPS)
+    return centre, inverse, moved_block * inverse
+
+
+def keep_stats(stats, where, centre, inverse):
+    stats[where, 0:1] = jnp.broadcast_to(centre, (16, 1))
+    stats[where, 1:2] = jnp.broadcast_to(inverse, (16, 1))
+
+
+def unit_of(block, stats, where):
+    return (block - stats[where, 0:1]) * stats[where, 1:2]
+
+
+def unit_back(grad, unit, inverse):
+    mean_grad = jnp.mean(grad, keepdims=True)
+    mean_both = jnp.mean(grad * unit, keepdims=True)
+    return (grad - mean_grad - unit * mean_both) * inverse
+
+
+def row_sum(block):
+    return jnp.sum(block, axis=1, keepdims=True)
+
+
+def first_conv(index, own, peer, par, w_own, w_part, w_peer, first, hidden, stats0, stats1, second, col, full):
+    half = index[0]
+    place_conv(full, index, w_own, w_part, w_peer)
+    masks = edge_masks(1)
+    for source, base in ((own, half * 256), (peer, (1 - half) * 256)):
+
+        def norm(group, carry, source=source, base=base):
+            where = rows(base + group * 16, 16)
+            centre, inverse, unit = group_stats(source[rows(group * 16, 16), :].astype(F32))
+            keep_stats(stats0, where, centre, inverse)
+            low = jax.nn.silu(unit * par[where, GAIN : GAIN + 1] + par[where, BIAS : BIAS + 1]).astype(BF)
+            first[where, :] = low
+            put_taps(col, masks, low.astype(F32), base + group * 16, 512, 0, 1)
+            return carry
+
+        lax.fori_loop(0, 16, norm, 0, unroll=2)
+    conv_dots(hidden, full, col, NN, lambda total, column: total + par[:, CONVB : CONVB + 1])
+
+    def again(group, carry):
+        where = rows(group * 16, 16)
+        centre, inverse, unit = group_stats(hidden[where, :])
+        keep_stats(stats1, where, centre, inverse)
+        normed = unit * par[where, GAIN + 1 : GAIN + 2] + par[where, BIAS + 1 : BIAS + 2]
+        pre = normed * (1.0 + par[where, SCALE : SCALE + 1]) + par[where, SHIFT : SHIFT + 1]
+        second[where, :] = jax.nn.silu(pre).astype(BF)
+        return carry
+
+    lax.fori_loop(0, 32, again, 0, unroll=2)
+
+
+def second_conv(index, source, own, peer, par, w_own, w_part, w_peer, resid, stats2, normed, col, full):
+    half = index[0]
+    place_conv(full, index, w_own, w_part, w_peer)
+    taps_of(col, edge_masks(1), source, 0, 512, 0, 1)
+    conv_dots(resid, full, col, NN, lambda total, column: total + par[:, CONVB + 1 : CONVB + 2])
+    for picture, base in ((own, half * 256), (peer, (1 - half) * 256)):
+
+        def norm(group, carry, picture=picture, base=base):
+            where = rows(base + group * 16, 16)
+            block = resid[where, :] + picture[rows(group * 16, 16), :].astype(F32)
+            resid[where, :] = block
+            centre, inverse, unit = group_stats(block)
+            keep_stats(stats2, where, centre, inverse)
+            normed[where, :] = (unit * par[where, GAIN + 2 : GAIN + 3] + par[where, BIAS + 2 : BIAS + 3]).astype(BF)
+            return carry
+
+        lax.fori_loop(0, 16, norm, 0, unroll=2)
+
+
+def place_square(full, index, own, peer):
+    half = index[0]
+    count = own.shape[0]
+    full[rows(half * count, count), :] = own[...]
+    full[rows((1 - half) * count, count), :] = peer[...]
+
+
+def attention(
+    index, normed, resid, stats2, par, cot_own, cot_peer, q_own, q_peer, p_own, p_peer,
+    mixed, grad_q, grad_k, grad_v, grad_out, grad_resid, grad_branch, small,
+    wq, wk, wv, wp, query, keys, values, grad_mixed, weights, grad_scores, grad_normed,
+):
+    half = index[0]
+    live = index[2] > 0
+    for which, full in enumerate((wq, wk, wv)):
+        place_square(full, index, q_own.at[which], q_peer.at[which])
+    place_square(wp, index, p_own, p_peer)
+    for cotangent, base in ((cot_own, half * 256), (cot_peer, (1 - half) * 256)):
+        grad_out[rows(base, 256), :] = jnp.where(live, cotangent[...], jnp.zeros_like(cotangent[...]))
+    for column in range(0, PIX, 512):
+        where = slice(column, column + 512)
+        query[:, where] = (mm(wq[...], normed[:, where]).astype(BF).astype(F32) * 0.125).astype(BF)
+        keys[:, where] = mm(wk[...], normed[:, where]).astype(BF)
+        values[:, where] = mm(wv[...], normed[:, where]).astype(BF)
+        grad_mixed[:, where] = mm(wp[...], grad_out[:, where]).astype(BF)
+
+    def head(number, carry):
+        where = rows(number * 64, 64)
+        q, k, v, g = query[where, :], keys[where, :], values[where, :], grad_mixed[where, :]
+        scores = mm(k.T, q)
+        expo = jnp.exp(scores - jnp.max(scores, axis=0, keepdims=True))
+        low = (expo * (1.0 / jnp.sum(expo, axis=0, keepdims=True))).astype(BF)
+        weights[...] = low
+        mix = mm(v, low)
+        mixed[where, :] = mix.astype(BF)
+        delta = jnp.sum(mix * g.astype(F32), axis=0, keepdims=True)
+        inner = (low.astype(F32) * (mm(v.T, g) - delta)).astype(BF)
+        grad_scores[...] = inner
+        grad_q[where, :] = (mm(k, inner) * 0.125).astype(BF)
+        grad_k[where, :] = mm(grad_scores[...], q.T).T.astype(BF)
+        grad_v[where, :] = mm(weights[...], g.T).T.astype(BF)
+        return carry
+
+    lax.fori_loop(0, HEADS, head, 0)
+    for column in range(0, PIX, 512):
+        where = slice(column, column + 512)
+        grad_normed[:, where] = (
+            mm(wq[...], grad_q[:, where], TN)
+            + mm(wk[...], grad_k[:, where], TN)
+            + mm(wv[...], grad_v[:, where], TN)
+        )
+
+    def back(group, carry):
+        where = rows(group * 16, 16)
+        unit = unit_of(resid[where, :], stats2, where)
+        grad = grad_normed[where, :]
+        outer = grad_out[where, :].astype(F32)
+        total = outer + unit_back(grad * par[where, GAIN + 2 : GAIN + 3], unit, stats2[where, 1:2])
+        low = total.astype(BF)
+        grad_resid[where, :] = total
+        grad_branch[where, :] = low
+        small[where, 0:1] = row_sum(grad * unit)
+        small[where, 1:2] = row_sum(grad)
+        small[where, 2:3] = row_sum(low.astype(F32))
+        small[where, 3:4] = row_sum(outer)
+        return carry
+
+    lax.fori_loop(0, 32, back, 0, unroll=2)
+
+
+def projections(
+    index, normed, resid, par, mixed, grad_q, grad_k, grad_v, grad_out, p_own, p_peer, block, grads, wp
+):
+    live = index[2] > 0
+    place_square(wp, index, p_own, p_peer)
+    for column in range(0, PIX, 512):
+        where = slice(column, column + 512)
+        total = resid[:, where] + mm(wp[...], mixed[:, where], TN) + par[:, PROJB : PROJB + 1]
+        block[:, where] = jnp.where(live, total, jnp.zeros_like(total)).astype(BF)
+    pairs = ((grad_q, normed), (grad_k, normed), (grad_v, normed), (mixed, grad_out))
+    for which, (left, right) in enumerate(pairs):
+        result = mm(left[...], right[...], NT).astype(BF)
+        for part in range(32):
+            plane, chunk = part // 16, part % 16
+            grads[chunk // 8, plane, chunk % 8, which] = result[part * 16 : (part + 1) * 16]
+
+
+def second_back(
+    index, grad_branch, hidden, stats1, par, w_own, w_part, w_peer, grad_hidden, small, col, full, grad_second
+):
+    place_conv(full, index, w_own, w_part, w_peer)
+    taps_of(col, edge_masks(-1), grad_branch, 0, 512, 0, -1)
+    conv_dots(grad_second, full, col, TN, lambda total, column: total)
+
+    def back(group, carry):
+        where = rows(group * 16, 16)
+        unit = unit_of(hidden[where, :], stats1, where)
+        gain = par[where, GAIN + 1 : GAIN + 2]
+        normed = unit * gain + par[where, BIAS + 1 : BIAS + 2]
+        scale = 1.0 + par[where, SCALE : SCALE + 1]
+        grad_pre = grad_second[where, :] * silu_slope(normed * scale + par[where, SHIFT : SHIFT + 1])
+        grad = grad_pre * scale
+        low = unit_back(grad * gain, unit, stats1[where, 1:2]).astype(BF)
+        grad_hidden[where, :] = low
+        small[where, 0:1] = row_sum(grad_pre * normed)
+        small[where, 1:2] = row_sum(grad_pre)
+        small[where, 2:3] = row_sum(grad * unit)
+        small[where, 3:4] = row_sum(grad)
+        small[where, 4:5] = row_sum(low.astype(F32))
+        return carry
+
+    lax.fori_loop(0, 32, back, 0, unroll=2)
+
+
+def first_back(
+    index, grad_hidden, own, peer, stats0, par, grad_resid, w_own, w_part, w_peer,
+    near, far, small, col, full, grad_first,
+):
+    half = index[0]
+    place_conv(full, index, w_own, w_part, w_peer)
+    taps_of(col, edge_masks(-1), grad_hidden, 0, 512, 0, -1)
+    conv_dots(grad_first, full, col, TN, lambda total, column: total)
+    for picture, base, dest in ((own, half * 256, near), (peer, (1 - half) * 256, far)):
+
+        def back(group, carry, picture=picture, base=base, dest=dest):
+            here = rows(group * 16, 16)
+            where = rows(base + group * 16, 16)
+            unit = unit_of(picture[here, :].astype(F32), stats0, where)
+            gain = par[where, GAIN : GAIN + 1]
+            grad = grad_first[where, :] * silu_slope(unit * gain + par[where, BIAS : BIAS + 1])
+            total = grad_resid[where, :] + unit_back(grad * gain, unit, stats0[where, 1:2])
+            dest[here, :] = total.astype(dest.dtype)
+            small[where, 0:1] = row_sum(grad * unit)
+            small[where, 1:2] = row_sum(grad)
+            return carry
+
+        lax.fori_loop(0, 16, back, 0, unroll=2)
+
+
+def weight_back(index, grad_own, grad_peer, source_own, source_peer, grads, col, turned):
+    masks = edge_masks(-1)
+    taps_of(col, masks, grad_own, 0, 256, 0, -1)
+    taps_of(col, masks, grad_peer, 0, 256, PIX, -1)
+    turned[:PIX, :] = source_own[...].T
+    turned[PIX:, :] = source_peer[...].T
+    for tap in range(9):
+        result = mm(col[tap * 256 : (tap + 1) * 256, :], turned[...]).astype(BF)
+        for part in range(16):
+            grads[part, tap] = result[part * 16 : (part + 1) * 16]
+
+
+def paired(
+    batch_size,
+    images,
+    timesteps,
+    classes,
+    live_count,
+    norm_gain,
+    norm_bias,
+    conv_weight,
+    conv_bias,
+    emb_weight,
+    emb_bias,
+    class_table,
+    qkv_weight,
+    proj_weight,
+    proj_bias,
+    cotangent,
+):
+    half = lax.axis_index("head")
+    place = lax.axis_index("batch")
+    core = place % 2
+    bits = batch_size.bit_length() - 1
+
+    def across(value):
+        return lax.ppermute(value, "head", [(0, 1), (1, 0)])
+
+    def over(value, bit):
+        return lax.ppermute(value, "batch", [(i, i ^ (1 << bit)) for i in range(batch_size)])
+
+    def pick(value, index):
+        return lax.dynamic_index_in_dim(value, index, 0, keepdims=False)
+
+    def by_half(near, far, axis):
+        return jnp.where(
+            half == 0,
+            jnp.concatenate([near, far], axis),
+            jnp.concatenate([far, near], axis),
+        )
+
+    def my_bit(bit):
+        return (place >> bit) & 1
+
+    def widen(value, bit):
+        peer = over(value, bit)
+        return jnp.where(
+            my_bit(bit) == 0, jnp.concatenate([value, peer]), jnp.concatenate([peer, value])
+        )
+
+    def halve(value, bit):
+        pair = value.reshape((2, value.shape[0] // 2) + value.shape[1:])
+        arrived = over(pick(pair, 1 - my_bit(bit)), bit)
+        return (pick(pair, my_bit(bit)).astype(F32) + arrived.astype(F32)).astype(BF)
+
+    image_own = pick(images, half)
+    image_peer = across(pick(images, 1 - half))
+    cot_own = pick(cotangent, half)
+    cot_peer = across(pick(cotangent, 1 - half))
+
+    def conv_parts(which):
+        own = conv_weight[which]
+        part = across(lax.dynamic_slice_in_dim(own, core * 128, 128, 1))
+        return own, part, over(part, 0)
+
+    weights0 = conv_parts(0)
+    weights1 = conv_parts(1)
+    q_peer = across(qkv_weight)
+    p_peer = across(proj_weight)
+
+    table_rows = jnp.stack([pick(class_table, classes[slot]) for slot in range(2)]).astype(F32)
+    emb_width = class_table.shape[1]
+    pre_embed = jnp.stack([features(timesteps[slot], emb_width) for slot in range(2)]) + table_rows
+    embed = jax.nn.silu(pre_embed)
+    dense = emb_weight.astype(F32)
+    mod = jnp.einsum("mce,be->bmc", dense, embed, precision=HIGH) + emb_bias[None]
+    params = jnp.concatenate([norm_gain, norm_bias, conv_bias, proj_bias[None]])
+    par_near = jnp.concatenate([params, pick(mod, half)])
+    par_far = across(jnp.concatenate([params, pick(mod, 1 - half)]))
+    par = by_half(par_near, par_far, 1).T
+
+    live = (half < live_count[0]).astype(jnp.int32)
+    scalars = jnp.stack([half, core, live]).astype(jnp.int32)
+    full_bf = out((512, PIX), BF)
+    full_f32 = out((512, PIX), F32)
+    half_bf = out((256, PIX), BF)
+    half_f32 = out((256, PIX), F32)
+    stats = out((512, 2), F32)
+    taps = pltpu.VMEM((9 * 512, PIX), BF)
+    conv_full = pltpu.VMEM((9, 512, 512), BF)
+    square = pltpu.VMEM((512, 512), BF)
+    wide_bf = pltpu.VMEM((512, PIX), BF)
+    wide_f32 = pltpu.VMEM((512, PIX), F32)
+    pixels = pltpu.VMEM((PIX, PIX), BF)
+    conv_flops = 2 * 9 * 512 * 512 * PIX
+
+    first, hidden, stats0, stats1, second = kernel_call(
+        first_conv, [full_bf, full_f32, stats, stats, full_bf], [taps, conv_full], conv_flops,
+        scalars, image_own, image_peer, par, *weights0,
+    )
+    resid, stats2, normed = kernel_call(
+        second_conv, [full_f32, stats, full_bf], [taps, conv_full], conv_flops,
+        scalars, second, image_own, image_peer, par, *weights1,
+    )
+    mixed, grad_q, grad_k, grad_v, grad_out, grad_resid, grad_branch, small2 = kernel_call(
+        attention,
+        [full_bf] * 5 + [full_f32, full_bf, out((512, 4), F32)],
+        [square] * 4 + [wide_bf] * 4 + [pixels] * 2 + [wide_f32],
+        4 * conv_flops,
+        scalars, normed, resid, stats2, par, cot_own, cot_peer, qkv_weight, q_peer, proj_weight, p_peer,
+    )
+    first_peer = across(first)
+    second_peer = across(second)
+
+    def halves(value):
+        pair = value.reshape(2, 256, PIX)
+        return pick(pair, half), across(pick(pair, 1 - half))
+
+    branch_own, branch_peer = halves(grad_branch)
+    grad_hidden, small1 = kernel_call(
+        second_back, [full_bf, out((512, 5), F32)], [taps, conv_full, wide_f32], conv_flops,
+        scalars, grad_branch, hidden, stats1, par, *weights1,
+    )
+    hidden_own, hidden_peer = halves(grad_hidden)
+    block, square_grads = kernel_call(
+        projections, [full_bf, out((2, 2, 8, 4, 16, 512), BF)], [square], conv_flops // 2,
+        scalars, normed, resid, par, mixed, grad_q, grad_k, grad_v, grad_out, proj_weight, p_peer,
+    )
+    block_own, block_peer = halves(block)
+    conv_grads = out((16, 9, 16, 512), BF)
+    tap_pair = pltpu.VMEM((9 * 256, 2 * PIX), BF)
+    turned = pltpu.VMEM((2 * PIX, 512), BF)
+
+    def weight_grad(grad_own, grad_peer, source, source_peer):
+        return kernel_call(
+            weight_back, [conv_grads], [tap_pair, turned], conv_flops,
+            scalars, grad_own, grad_peer, source, source_peer,
+        )[0]
+
+    conv_grad1 = weight_grad(branch_own, branch_peer, second, second_peer)
+    conv_grad0 = weight_grad(hidden_own, hidden_peer, first, first_peer)
+    near, far, small0 = kernel_call(
+        first_back, [half_f32, half_bf, out((512, 2), F32)], [taps, conv_full, wide_f32], conv_flops,
+        scalars, grad_hidden, image_own, image_peer, stats0, par, grad_resid, *weights0,
+    )
+    far = across(far).astype(F32)
+
+    def reduce_conv(value):
+        for bit in range(bits):
+            value = halve(value, bit)
+        for bit in reversed(range(bits)):
+            value = widen(value, bit)
+        return value.transpose(1, 0, 2, 3).reshape(9, 256, 512).astype(F32)
+
+    conv_total1 = reduce_conv(conv_grad1)
+    conv_total0 = reduce_conv(conv_grad0)
+
+    squares = halve(square_grads, 0)[0]
+    keep_part, send_part = pick(squares, half), pick(squares, 1 - half)
+    squares = (keep_part.astype(F32) + across(send_part).astype(F32)).astype(BF)
+    for bit in range(1, bits):
+        squares = halve(squares, bit)
+    for bit in reversed(range(bits)):
+        squares = widen(squares, bit)
+    squares = squares.transpose(1, 0, 2, 3).reshape(4, 256, 512).astype(F32)
+
+    small = jnp.concatenate([small0, small1, small2], 1).T.reshape(11, 2, 256).transpose(1, 0, 2)
+    small_own, small_peer = pick(small, half), across(pick(small, 1 - half))
+    sums = small_own + small_peer
+    for bit in range(bits):
+        sums = sums + over(sums, bit)
+    emb_own, emb_peer = small_own[2:4], small_peer[2:4]
+    emb_grads = by_half(emb_own[None], emb_peer[None], 0)
+    pre_all = pre_embed
+    ids = classes
+    for bit in range(bits):
+        emb_grads = widen(emb_grads, bit)
+        pre_all = widen(pre_all, bit)
+        ids = widen(ids, bit)
+    emb_total = jnp.einsum("bmc,be->mce", emb_grads, jax.nn.silu(pre_all), precision=HIGH)
+    rows_part = jnp.einsum("bmc,mce->be", emb_grads, dense, precision=HIGH)
+    class_rows = (rows_part + across(rows_part)) * silu_slope(pre_all)
+    chosen = (lax.iota(jnp.int32, class_table.shape[0])[:, None] == ids[None, :]).astype(F32)
+    table_total = jnp.dot(chosen, class_rows, precision=HIGH)
+    return (
+        by_half(block_own[None], block_peer[None], 0),
+        by_half(near[None], far[None], 0),
+        jnp.stack([sums[0], sums[4], sums[7]]),
+        jnp.stack([sums[1], sums[5], sums[8]]),
+        jnp.stack([conv_total0, conv_total1]),
+        jnp.stack([sums[6], sums[9]]),
+        emb_total,
+        sums[2:4],
+        table_total,
+        squares[:3],
+        squares[3],
+        sums[10],
+    )
+
+
 def solution(mesh):
     in_specs = (
         P("batch", "head", None),
@@ -424,4 +939,8 @@
         P("head", None),
         P("head"),
     )
-    return jax.shard_map(shards, mesh=mesh, in_specs=in_specs, out_specs=out_specs, check_vma=False)
+    body = shards
+    batch_size = mesh.shape["batch"]
+    if mesh.shape["head"] == 2 and batch_size in (8, 16):
+        body = functools.partial(paired, batch_size)
+    return jax.shard_map(body, mesh=mesh, in_specs=in_specs, out_specs=out_specs, check_vma=False)

time: 1010 us -> 470 us (0.47)
  waiting for transfers between devices: 433 us -> 168 us
  matrix products: 263 us -> 8.67 us
  Pallas kernels: 0 us -> 178 us
  other arithmetic: 149 us -> 15 us
  local copies, waits for them, and re-layouts: 88.6 us -> 32.4 us
  starting transfers between devices: 3.39 us -> 56.1 us
  blocking collectives: 36 us -> 0 us
  loops' own time: 12.6 us -> 0 us
    dot_general x144 -> x4, matrix products: 263 us -> 8.67 us  [the longest x1 3.99 us: paired(): table_total = jnp.dot(chosen, class_rows, precision=HIGH)]
    psum x2 -> x0, waiting for transfers between devices: 245 us -> none  [the longest x1 135 us: shards(): table_total = lax.psum(table_acc, ('batch', 'head'))]
    pallas_call x0 -> x8, Pallas kernels: none -> 178 us  [kernel_call(): pl.pallas_call(kernel, out_shape=outs, in_specs=[SMEM] + [VMEM] * len(arg...]
    ppermute x0 -> x58, waiting for transfers between devices: none -> 168 us  [the longest x42 106 us: over(): lax.ppermute(value, 'batch', [(i, i ^ 1 << bit) for i in range(batch_size)])]
    all_gather x8 -> x0, waiting for transfers between devices: 107 us -> none  [the longest x6 107 us: gather_channels(): return lax.all_gather(rows_low, 'head', axis=0, tiled=True)]
    reduce_scatter x8 -> x0, waiting for transfers between devices: 80.9 us -> none  [the longest x4 40.8 us: input_grad(): lax.psum_scatter(conv_transpose(weight_cols, grad_rows, grid_side).astype...]
    convert_element_type x27 -> x16, other arithmetic: 60.7 us -> 3.5 us  [the longest x12 2.25 us: halve(): (pick(pair, my_bit(bit)).astype(F32) + arrived.astype(F32)).astype(BF)]
    ppermute x0 -> x58, starting transfers between devices: none -> 56.1 us  [the longest x42 36.3 us: over(): lax.ppermute(value, 'batch', [(i, i ^ 1 << bit) for i in range(batch_size)])]
  transfers between devices with their start and end apart: 18 -> 58, of which waited for: 12 -> 29; matrix products, arithmetic and copies ran while one was open for 19% -> 9% of each run, Pallas kernels for 0% -> 38%
where the time goes in v1:
time: 470 us; the launch traced here: 466 us
  Pallas kernels  178 us (38%)
  waiting for transfers between devices  168 us (36%)
  starting transfers between devices  56.1 us (12%)
  local copies, waits for them, and re-layouts  32.4 us (7%)
  other arithmetic  15 us (3%)
  matrix products  8.67 us (2%)
  between operations  7.52 us (2%)
    pallas_call x8, Pallas kernels, kernel_call(): pl.pallas_call(kernel, out_shape=outs, in_specs=[SMEM] + [VMEM] * len(arg...  178 us
    ppermute x42, waiting for transfers between devices, over(): lax.ppermute(value, 'batch', [(i, i ^ 1 << bit) for i in range(batch_size)])  106 us
    ppermute x16, waiting for transfers between devices, across(): return lax.ppermute(value, 'head', [(0, 1), (1, 0)])  62.1 us
    ppermute x42, starting transfers between devices, over(): lax.ppermute(value, 'batch', [(i, i ^ 1 << bit) for i in range(batch_size)])  36.3 us
    ppermute x16, starting transfers between devices, across(): return lax.ppermute(value, 'head', [(0, 1), (1, 0)])  19.8 us
    squeeze x16, local copies, waits for them, and re-layouts, pick(): return lax.dynamic_index_in_dim(value, index, 0, keepdims=False)  10.5 us
  transfers between devices with their start and end apart: 58, of which 29 were waited for; matrix products, arithmetic and copies ran while one was open for 9% of the time, Pallas kernels for 38%

profile of v1, /device:TPU:0, one launch (start us, length us, event | category | flops | bytes accessed | tf_op | source)
XLA Modules:
  0.0 465.7 jit_solution(11061289411775654873)
XLA Ops:
  0.7 5.9 %fusion.44 = (bf16[1,9,256,512]{3,2,1,0:T(8,128)(2,1)S(1)}, bf16[9,256,512]{2,1,0:T(8,128)(2,1)}, bf16[9,256,512]{2,1,0:T(8,128)(2,1)}, bf16[1,9,256,512]{3,2,1,0:T(8,128)(2,1)}) fusion(bf16[2,9,256,512]{3,2,1,0:T(8,128)(2,1)} %param.21), kind=kLoop, calls=%fused_computation.144 | loop fusion | bytes 14155776 | tf_op jit(solution)/shard_map/slice | solution.py:771
  9.0 3.0 collective-permute-start.2
  27.8 11.4 %collective-permute-done.2.w_part = bf16[9,128,512]{2,1,0:T(8,128)(2,1)} collective-permute-done((bf16[9,128,512]{2,1,0:T(8,128)(2,1)}, bf16[9,128,512]{2,1,0:T(8,128)(2,1)}, u32[]{:S(2)}, u32[]{:S(2)}) %collective-permute-start.2) | collective-permute-done | bytes 1179680 | tf_op jit(solution)/shard_map/ppermute | solution.py:736
  47.2 3.0 collective-permute-start.47
  53.6 10.8 %collective-permute-done.4.w_part = bf16[9,128,512]{2,1,0:T(8,128)(2,1)} collective-permute-done((bf16[9,128,512]{2,1,0:T(8,128)(2,1)}, bf16[9,128,512]{2,1,0:T(8,128)(2,1)}, u32[]{:S(2)}, u32[]{:S(2)}) %collective-permute-start.4) | collective-permute-done | bytes 1179680 | tf_op jit(solution)/shard_map/ppermute | solution.py:736
  78.1 2.6 collective-permute-start.43
  80.7 27.2 %shard_map.238 = (bf16[512,1024]{1,0:T(8,128)(2,1)}, f32[512,1024]{1,0:T(8,128)}, f32[512,2]{1,0:T(8,128)}, f32[512,2]{1,0:T(8,128)}, bf16[512,1024]{1,0:T(8,128)(2,1)}) custom-call(s32[3]{0:T(128)} %pad_add_fusion.index, bf16[256,1024]{1,0:T(8,128)(2,1)} %get-tuple-element.73.own, bf16[256,1024]{1,0:T(8,128)(2,1)} %collective-permute-done.peer, ...), custom_call_target="tpu_custom_call" | custom-call | flops 4831838208 | bytes 9992192 | tf_op jit(solution)/shard_map/pallas_call | solution.py:417
  107.8 23.0 %shard_map.239 = (f32[512,1024]{1,0:T(8,128)}, f32[512,2]{1,0:T(8,128)}, bf16[512,1024]{1,0:T(8,128)(2,1)}) custom-call(s32[3]{0:T(128)} %pad_add_fusion.index, bf16[512,1024]{1,0:T(8,128)(2,1)} %get-tuple-element.35.source.source_own, bf16[256,1024]{1,0:T(8,128)(2,1)} %get-tuple-element.73.own, bf16[256,1024]{1,0:T(8,128)(2,1)} %collective-permute-done.peer, ...), custom_call_target="tpu_custom_call" | custom-call | flops 4831838208 | bytes 9988096 | tf_op jit(solution)/shard_map/pallas_call | solution.py:417
  131.8 47.0 %shard_map.240 = (bf16[512,1024]{1,0:T(8,128)(2,1)}, bf16[512,1024]{1,0:T(8,128)(2,1)}, bf16[512,1024]{1,0:T(8,128)(2,1)}, bf16[512,1024]{1,0:T(8,128)(2,1)}, bf...) custom-call(s32[3]{0:T(128)} %pad_add_fusion.index, ...), custom_call_target="tpu_custom_call" | custom-call | flops 19327352832 | bytes 14714880 | tf_op jit(solution)/shard_map/pallas_call | solution.py:417
  178.7 7.9 %shard_map.241 = (bf16[512,1024]{1,0:T(8,128)(2,1)}, bf16[2,2,8,4,16,512]{5,4,3,2,1,0:T(8,128)(2,1)}) custom-call(s32[3]{0:T(128)} %pad_add_fusion.index, bf16[512,1024]{1,0:T(8,128)(2,1)} %get-tuple-element.36.normed, f32[512,1024]{1,0:T(8,128)} %get-tuple-element.37.resid, f32[512,11]{1,0:T(8,128)} %select_bitcast_fusion.par, ...), custom_call_target="tpu_custom_call" | custom-call | flops 2415919104 | bytes 12081152 | tf_op jit(solution)/shard_map/pallas_call | solution.py:417
  188.1 22.1 %shard_map.242 = (bf16[512,1024]{1,0:T(8,128)(2,1)}, f32[512,5]{1,0:T(8,128)}) custom-call(s32[3]{0:T(128)} %pad_add_fusion.index, bf16[512,1024]{1,0:T(8,128)(2,1)} %get-tuple-element.45.grad_branch, f32[512,1024]{1,0:T(8,128)} %get-tuple-element.46.hidden, f32[512,2]{1,0:T(8,128)} %get-tuple-element.47.stats1, f32[512,11]{1,0:T(8,128)} %select_bitcast_fusion.par, ...), custom_call_target="tpu_custom_call" | custom-call | flops 4831838208 | bytes 8949760 | tf_op jit(solution)/shard_map/pallas_call | solution.py:417
  210.2 21.3 %shard_map.243 = (f32[256,1024]{1,0:T(8,128)}, bf16[256,1024]{1,0:T(8,128)(2,1)}, f32[512,2]{1,0:T(8,128)}) custom-call(s32[3]{0:T(128)} %pad_add_fusion.index, bf16[512,1024]{1,0:T(8,128)(2,1)} %get-tuple-element.48.grad_hidden, bf16[256,1024]{1,0:T(8,128)(2,1)} %get-tuple-element.73.own, bf16[256,1024]{1,0:T(8,128)(2,1)} %collective-permute-done.peer, ...), custom_call_target="tpu_custom_call" | custom-call | flops 4831838208 | bytes 10516480 | tf_op jit(solution)/shard_map/pallas_call | solution.py:417
  251.4 4.3 collective-permute-done.15
  258.8 38.4 %collective-permute-done.16.grad_peer = bf16[256,1024]{1,0:T(8,128)(2,1)S(1)} collective-permute-done((bf16[256,1024]{1,0:T(8,128)(2,1)S(1)}, bf16[256,1024]{1,0:T(8,128)(2,1)S(1)}, u32[]{:S(2)}, u32[]{:S(2)}) %collective-permute-start.16) | collective-permute-done | bytes 524320 | tf_op jit(solution)/shard_map/ppermute | solution.py:736
  299.7 14.7 %shard_map.244 = bf16[16,9,16,512]{3,2,1,0:T(8,128)(2,1)} custom-call(s32[3]{0:T(128)} %pad_add_fusion.index, bf16[256,1024]{1,0:T(8,128)(2,1)} %get-tuple-element.65.grad_own, bf16[256,1024]{1,0:T(8,128)(2,1)} %copy-done.20, bf16[512,1024]{1,0:T(8,128)(2,1)} %get-tuple-element.56.source_own, bf16[512,1024]{1,0:T(8,128)(2,1)} %copy-done.18), custom_call_target="tpu_custom_call" | custom-call | flops 4831838208 | bytes 5505024 | tf_op jit(solution)/shard_map/pallas_call | solution.py:417
  316.5 14.9 %shard_map.245 = bf16[16,9,16,512]{3,2,1,0:T(8,128)(2,1)} custom-call(s32[3]{0:T(128)} %pad_add_fusion.index, bf16[256,1024]{1,0:T(8,128)(2,1)} %get-tuple-element.67.grad_own, bf16[256,1024]{1,0:T(8,128)(2,1)} %copy-done.21, bf16[512,1024]{1,0:T(8,128)(2,1)} %get-tuple-element.35.source.source_own, bf16[512,1024]{1,0:T(8,128)(2,1)} %collective-permute-done.27.source_peer), custom_call_target="tpu_custom_call" | custom-call | flops 4831838208 | bytes 5505024 | tf_op jit(solution)/shard_map/pallas_call | solution.py:417
  337.1 4.8 %collective-permute-done.51 = bf16[4,4,16,512]{3,2,1,0:T(8,128)(2,1)S(1)} collective-permute-done((bf16[4,4,16,512]{3,2,1,0:T(8,128)(2,1)S(1)}, bf16[4,4,16,512]{3,2,1,0:T(8,128)(2,1)S(1)}, u32[]{:S(2)}, u32[]{:S(2)}) %collective-permute-start.51) | collective-permute-done | bytes 262176 | tf_op jit(solution)/shard_map/ppermute | solution.py:739
  349.7 11.9 %collective-permute-done.19 = bf16[4,9,16,512]{3,2,1,0:T(8,128)(2,1)S(1)} collective-permute-done((bf16[4,9,16,512]{3,2,1,0:T(8,128)(2,1)S(1)}, bf16[4,9,16,512]{3,2,1,0:T(8,128)(2,1)S(1)}, u32[]{:S(2)}, u32[]{:S(2)}) %collective-permute-start.19) | collective-permute-done | bytes 589856 | tf_op jit(solution)/shard_map/ppermute | solution.py:739
  362.4 10.0 %collective-permute-done.29 = bf16[4,9,16,512]{3,2,1,0:T(8,128)(2,1)S(1)} collective-permute-done((bf16[4,9,16,512]{3,2,1,0:T(8,128)(2,1)S(1)}, bf16[4,9,16,512]{3,2,1,0:T(8,128)(2,1)S(1)}, u32[]{:S(2)}, u32[]{:S(2)}) %collective-permute-start.29) | collective-permute-done | bytes 589856 | tf_op jit(solution)/shard_map/ppermute | solution.py:739
  373.7 9.3 %collective-permute-done.30 = bf16[2,9,16,512]{3,2,1,0:T(8,128)(2,1)S(1)} collective-permute-done((bf16[2,9,16,512]{3,2,1,0:T(8,128)(2,1)S(1)}, bf16[2,9,16,512]{3,2,1,0:T(8,128)(2,1)S(1)}, u32[]{:S(2)}, u32[]{:S(2)}) %collective-permute-start.30) | collective-permute-done | bytes 294944 | tf_op jit(solution)/shard_map/ppermute | solution.py:739
  383.3 3.0 collective-permute-start.22
  386.3 9.3 %collective-permute-done.31 = bf16[1,9,16,512]{3,2,1,0:T(8,128)(2,1)S(1)} collective-permute-done((bf16[1,9,16,512]{3,2,1,0:T(8,128)(2,1)S(1)}, bf16[1,9,16,512]{3,2,1,0:T(8,128)(2,1)S(1)}, u32[]{:S(2)}, u32[]{:S(2)}) %collective-permute-start.31) | collective-permute-done | bytes 147488 | tf_op jit(solution)/shard_map/ppermute | solution.py:739
  395.7 5.3 %collective-permute-done.22 = bf16[1,9,16,512]{3,2,1,0:T(8,128)(2,1)S(1)} collective-permute-done((bf16[1,9,16,512]{3,2,1,0:T(8,128)(2,1)S(1)}, bf16[1,9,16,512]{3,2,1,0:T(8,128)(2,1)S(1)}, u32[]{:S(2)}, u32[]{:S(2)}) %collective-permute-start.22) | collective-permute-done | bytes 147488 | tf_op jit(solution)/shard_map/ppermute | solution.py:739
  401.0 3.8 collective-permute-done.32
  407.0 7.7 %collective-permute-done.23 = bf16[2,9,16,512]{3,2,1,0:T(8,128)(2,1)S(1)} collective-permute-done((bf16[2,9,16,512]{3,2,1,0:T(8,128)(2,1)S(1)}, bf16[2,9,16,512]{3,2,1,0:T(8,128)(2,1)S(1)}, u32[]{:S(2)}, u32[]{:S(2)}) %collective-permute-start.23) | collective-permute-done | bytes 294944 | tf_op jit(solution)/shard_map/ppermute | solution.py:739
  414.8 5.9 %collective-permute-done.33 = bf16[2,9,16,512]{3,2,1,0:T(8,128)(2,1)S(1)} collective-permute-done((bf16[2,9,16,512]{3,2,1,0:T(8,128)(2,1)S(1)}, bf16[2,9,16,512]{3,2,1,0:T(8,128)(2,1)S(1)}, u32[]{:S(2)}, u32[]{:S(2)}) %collective-permute-start.33) | collective-permute-done | bytes 294944 | tf_op jit(solution)/shard_map/ppermute | solution.py:739
  423.0 3.2 fusion.13
  428.3 4.4 collective-permute-done.55
  433.7 3.3 collective-permute-done.24
  438.7 10.9 %collective-permute-done.34 = bf16[4,9,16,512]{3,2,1,0:T(8,128)(2,1)S(1)} collective-permute-done((bf16[4,9,16,512]{3,2,1,0:T(8,128)(2,1)S(1)}, bf16[4,9,16,512]{3,2,1,0:T(8,128)(2,1)S(1)}, u32[]{:S(2)}, u32[]{:S(2)}) %collective-permute-start.34) | collective-permute-done | bytes 589856 | tf_op jit(solution)/shard_map/ppermute | solution.py:739
  450.4 4.0 fusion.10
  461.1 4.4 maximum_convert_fusion
  (244 shorter events, 99.7 us)
Async XLA Ops:
  9.0 30.1 %collective-permute-start.2 = (bf16[9,128,512]{2,1,0:T(8,128)(2,1)}, bf16[9,128,512]{2,1,0:T(8,128)(2,1)}, u32[]{:S(2)}, u32[]{:S(2)}) collective-permute-start(bf16[9,128,512]{2,1,0:T(8,128)(2,1)} %dynamic-slice_bitcast_fusion.3), channel_id=1, source_target_pairs={{0,1},{1,0},{2,3},{3,2},{4,5},{5,4},{6,7},{7,6},{8,9},{9,8},{10,11... | collective-permute-start | bytes 3538952 | tf_op jit(solution)/shard_map/ppermute | solution.py:736
  13.2 51.3 %collective-permute-start.4 = (bf16[9,128,512]{2,1,0:T(8,128)(2,1)}, bf16[9,128,512]{2,1,0:T(8,128)(2,1)}, u32[]{:S(2)}, u32[]{:S(2)}) collective-permute-start(bf16[9,128,512]{2,1,0:T(8,128)(2,1)} %dynamic-slice_bitcast_fusion.2), channel_id=1, source_target_pairs={{0,1},{1,0},{2,3},{3,2},{4,5},{5,4},{6,7},{7,6},{8,9},{9,8},{10,11... | collective-permute-start | bytes 3538952 | tf_op jit(solution)/shard_map/ppermute | solution.py:736
  13.2 26.6 %collective-permute-start.44 = (s32[2]{0:T(128)S(1)}, s32[2]{0:T(128)S(1)}, u32[]{:S(2)}, u32[]{:S(2)}) collective-permute-start(s32[2]{0:T(128)S(1)} %copy-done.13), channel_id=1, source_target_pairs={{0,2},{2,0},{4,6},{6,4},{8,10},{10,8},{12,14},{14,12},{16,18},{18,... | collective-permute-start | bytes 32 | tf_op jit(solution)/shard_map/ppermute | solution.py:739
  20.5 44.0 %collective-permute-start.40 = (f32[2,1024]{1,0:T(2,128)S(1)}, f32[2,1024]{1,0:T(2,128)S(1)}, u32[]{:S(2)}, u32[]{:S(2)}) collective-permute-start(f32[2,1024]{1,0:T(2,128)S(1)} %maximum_add_fusion), channel_id=1, source_target_pairs={{0,2},{2,0},{4,6},{6,4},{8,10},{10,8},{12,14},{14,12},{16,18},{18,... | collective-permute-start | bytes 24584 | tf_op jit(solution)/shard_map/ppermute | solution.py:739
  22.1 44.5 %collective-permute-start.1 = (f32[11,256]{1,0:T(8,128)S(1)}, f32[11,256]{1,0:T(8,128)S(1)}, u32[]{:S(2)}, u32[]{:S(2)}) collective-permute-start(f32[11,256]{1,0:T(8,128)S(1)} %concatenate.203), channel_id=1, source_target_pairs={{0,1},{1,0},{2,3},{3,2},{4,5},{5,4},{6,7},{7,6},{8,9},{9,8},{10,11... | collective-permute-start | bytes 33800 | tf_op jit(solution)/shard_map/ppermute | solution.py:736
  39.1 38.9 %collective-permute-start.3 = (bf16[9,128,512]{2,1,0:T(8,128)(2,1)}, bf16[9,128,512]{2,1,0:T(8,128)(2,1)}, u32[]{:S(2)}, u32[]{:S(2)}) collective-permute-start(bf16[9,128,512]{2,1,0:T(8,128)(2,1)} %collective-permute-done.2.w_part), channel_id=1, source_target_pairs={{0,2},{2,0},{4,6},{6,4},{8,10},{10,8},{12,14},{14,12},{16,18},{18,... | collective-permute-start | bytes 3538952 | tf_op jit(solution)/shard_map/ppermute | solution.py:739
  51.8 24.2 %collective-permute-start = (bf16[256,1024]{1,0:T(8,128)(2,1)S(1)}, bf16[256,1024]{1,0:T(8,128)(2,1)}, u32[]{:S(2)}, u32[]{:S(2)}) collective-permute-start(bf16[256,1024]{1,0:T(8,128)(2,1)S(1)} %get-tuple-element.72), channel_id=1, source_target_pairs={{0,1},{1,0},{2,3},{3,2},{4,5},{5,4},{6,7},{7,6},{8,9},{9,8},{10,11... | collective-permute-start | bytes 1572872 | tf_op jit(solution)/shard_map/ppermute | solution.py:736
  64.4 43.4 %collective-permute-start.5 = (bf16[9,128,512]{2,1,0:T(8,128)(2,1)}, bf16[9,128,512]{2,1,0:T(8,128)(2,1)}, u32[]{:S(2)}, u32[]{:S(2)}) collective-permute-start(bf16[9,128,512]{2,1,0:T(8,128)(2,1)} %collective-permute-done.4.w_part), channel_id=1, source_target_pairs={{0,2},{2,0},{4,6},{6,4},{8,10},{10,8},{12,14},{14,12},{16,18},{18,... | collective-permute-start | bytes 3538952 | tf_op jit(solution)/shard_map/ppermute | solution.py:739
  64.5 66.3 %collective-permute-start.6 = (bf16[256,1024]{1,0:T(8,128)(2,1)S(1)}, bf16[256,1024]{1,0:T(8,128)(2,1)}, u32[]{:S(2)}, u32[]{:S(2)}) collective-permute-start(bf16[256,1024]{1,0:T(8,128)(2,1)S(1)} %get-tuple-element.70), channel_id=1, source_target_pairs={{0,1},{1,0},{2,3},{3,2},{4,5},{5,4},{6,7},{7,6},{8,9},{9,8},{10,11... | collective-permute-start | bytes 1572872 | tf_op jit(solution)/shard_map/ppermute | solution.py:736
  74.4 56.4 %collective-permute-start.8 = (bf16[256,512]{1,0:T(8,128)(2,1)}, bf16[256,512]{1,0:T(8,128)(2,1)S(1)}, u32[]{:S(2)}, u32[]{:S(2)}) collective-permute-start(bf16[256,512]{1,0:T(8,128)(2,1)} %p_own.3), channel_id=1, source_target_pairs={{0,1},{1,0},{2,3},{3,2},{4,5},{5,4},{6,7},{7,6},{8,9},{9,8},{10,11... | collective-permute-start | bytes 786440 | tf_op jit(solution)/shard_map/ppermute | solution.py:736
  76.0 54.8 %collective-permute-start.7 = (bf16[3,256,512]{2,1,0:T(8,128)(2,1)}, bf16[3,256,512]{2,1,0:T(8,128)(2,1)S(1)}, u32[]{:S(2)}, u32[]{:S(2)}) collective-permute-start(bf16[3,256,512]{2,1,0:T(8,128)(2,1)} %q_own.1), channel_id=1, source_target_pairs={{0,1},{1,0},{2,3},{3,2},{4,5},{5,4},{6,7},{7,6},{8,9},{9,8},{10,11... | collective-permute-start | bytes 2359304 | tf_op jit(solution)/shard_map/ppermute | solution.py:736
  78.1 344.3 %collective-permute-start.43 = (f32[16,1024]{1,0:T(8,128)S(1)}, f32[16,1024]{1,0:T(8,128)S(1)}, u32[]{:S(2)}, u32[]{:S(2)}) collective-permute-start(f32[16,1024]{1,0:T(8,128)S(1)} %maximum_select_fusion.18), channel_id=1, source_target_pairs={{0,16},{2,18},{4,20},{6,22},{8,24},{10,26},{12,28},{14,30},{16,0},... | collective-permute-start | bytes 196616 | tf_op jit(solution)/shard_map/ppermute | solution.py:739
  188.0 69.8 %collective-permute-start.49 = (bf16[1,2,8,4,16,512]{5,4,3,2,1,0:T(8,128)(2,1)S(1)}, bf16[1,2,8,4,16,512]{5,4,3,2,1,0:T(8,128)(2,1)S(1)}, u32[]{:S(2)}, u32[]{:S(2)}) collective-permute-start(bf16[1,2,8,4,16,512]{5,4,3,2,1,0:T(8,128)(2,1)S(1)} %constant_dynamic-slice_fusion.3), channel_id=1, source_target_pairs={{0,2},{2,0},{4,6},{6,4},{8,10},{10,8},{12,14},{14,12},{16,18},{18,... | collective-permute-start | bytes 3145736 | tf_op jit(solution)/shard_map/ppermute | solution.py:739
  237.5 61.2 %collective-permute-start.17 = (bf16[512,1024]{1,0:T(8,128)(2,1)S(1)}, bf16[512,1024]{1,0:T(8,128)(2,1)S(1)}, u32[]{:S(2)}, u32[]{:S(2)}) collective-permute-start(bf16[512,1024]{1,0:T(8,128)(2,1)S(1)} %copy-done.17), channel_id=1, source_target_pairs={{0,1},{1,0},{2,3},{3,2},{4,5},{5,4},{6,7},{7,6},{8,9},{9,8},{10,11... | collective-permute-start | bytes 3145736 | tf_op jit(solution)/shard_map/ppermute | solution.py:736
  250.5 65.4 %collective-permute-start.27 = (bf16[512,1024]{1,0:T(8,128)(2,1)}, bf16[512,1024]{1,0:T(8,128)(2,1)}, u32[]{:S(2)}, u32[]{:S(2)}) collective-permute-start(bf16[512,1024]{1,0:T(8,128)(2,1)} %get-tuple-element.35.source.source_own), channel_id=1, source_target_pairs={{0,1},{1,0},{2,3},{3,2},{4,5},{5,4},{6,7},{7,6},{8,9},{9,8},{10,11... | collective-permute-start | bytes 3145736 | tf_op jit(solution)/shard_map/ppermute | solution.py:736
  255.7 41.5 %collective-permute-start.16 = (bf16[256,1024]{1,0:T(8,128)(2,1)S(1)}, bf16[256,1024]{1,0:T(8,128)(2,1)S(1)}, u32[]{:S(2)}, u32[]{:S(2)}) collective-permute-start(bf16[256,1024]{1,0:T(8,128)(2,1)S(1)} %get-tuple-element.64), channel_id=1, source_target_pairs={{0,1},{1,0},{2,3},{3,2},{4,5},{5,4},{6,7},{7,6},{8,9},{9,8},{10,11... | collective-permute-start | bytes 1572872 | tf_op jit(solution)/shard_map/ppermute | solution.py:736
  257.8 57.9 %collective-permute-start.26 = (bf16[256,1024]{1,0:T(8,128)(2,1)}, bf16[256,1024]{1,0:T(8,128)(2,1)S(1)}, u32[]{:S(2)}, u32[]{:S(2)}) collective-permute-start(bf16[256,1024]{1,0:T(8,128)(2,1)} %get-tuple-element.66), channel_id=1, source_target_pairs={{0,1},{1,0},{2,3},{3,2},{4,5},{5,4},{6,7},{7,6},{8,9},{9,8},{10,11... | collective-permute-start | bytes 1572872 | tf_op jit(solution)/shard_map/ppermute | solution.py:736
  297.2 158.5 %collective-permute-start.10 = (bf16[256,1024]{1,0:T(8,128)(2,1)}, bf16[256,1024]{1,0:T(8,128)(2,1)S(1)}, u32[]{:S(2)}, u32[]{:S(2)}) collective-permute-start(bf16[256,1024]{1,0:T(8,128)(2,1)} %get-tuple-element.52), channel_id=1, source_target_pairs={{0,1},{1,0},{2,3},{3,2},{4,5},{5,4},{6,7},{7,6},{8,9},{9,8},{10,11... | collective-permute-start | bytes 1572872 | tf_op jit(solution)/shard_map/ppermute | solution.py:736
  298.7 34.2 %collective-permute-start.50 = (bf16[8,4,16,512]{3,2,1,0:T(8,128)(2,1)S(1)}, bf16[8,4,16,512]{3,2,1,0:T(8,128)(2,1)S(1)}, u32[]{:S(2)}, u32[]{:S(2)}) collective-permute-start(bf16[8,4,16,512]{3,2,1,0:T(8,128)(2,1)S(1)} %dynamic-slice_bitcast_fusion.6), channel_id=1, source_target_pairs={{0,1},{1,0},{2,3},{3,2},{4,5},{5,4},{6,7},{7,6},{8,9},{9,8},{10,11... | collective-permute-start | bytes 1572872 | tf_op jit(solution)/shard_map/ppermute | solution.py:736
  315.7 27.4 %collective-permute-start.18 = (bf16[8,9,16,512]{3,2,1,0:T(8,128)(2,1)S(1)}, bf16[8,9,16,512]{3,2,1,0:T(8,128)(2,1)S(1)}, u32[]{:S(2)}, u32[]{:S(2)}) collective-permute-start(bf16[8,9,16,512]{3,2,1,0:T(8,128)(2,1)S(1)} %dynamic-slice_bitcast_fusion.1), channel_id=1, source_target_pairs={{0,2},{2,0},{4,6},{6,4},{8,10},{10,8},{12,14},{14,12},{16,18},{18,... | collective-permute-start | bytes 3538952 | tf_op jit(solution)/shard_map/ppermute | solution.py:739
  332.8 12.5 %collective-permute-start.28 = (bf16[8,9,16,512]{3,2,1,0:T(8,128)(2,1)S(1)}, bf16[8,9,16,512]{3,2,1,0:T(8,128)(2,1)S(1)}, u32[]{:S(2)}, u32[]{:S(2)}) collective-permute-start(bf16[8,9,16,512]{3,2,1,0:T(8,128)(2,1)S(1)} %dynamic-slice_bitcast_fusion), channel_id=1, source_target_pairs={{0,2},{2,0},{4,6},{6,4},{8,10},{10,8},{12,14},{14,12},{16,18},{18,... | collective-permute-start | bytes 3538952 | tf_op jit(solution)/shard_map/ppermute | solution.py:739
  341.9 112.6 %collective-permute-start.9 = (bf16[256,1024]{1,0:T(8,128)(2,1)S(1)}, bf16[256,1024]{1,0:T(8,128)(2,1)S(1)}, u32[]{:S(2)}, u32[]{:S(2)}) collective-permute-start(bf16[256,1024]{1,0:T(8,128)(2,1)S(1)} %copy-done.8), channel_id=1, source_target_pairs={{0,1},{1,0},{2,3},{3,2},{4,5},{5,4},{6,7},{7,6},{8,9},{9,8},{10,11... | collective-permute-start | bytes 1572872 | tf_op jit(solution)/shard_map/ppermute | solution.py:736
  345.3 16.3 %collective-permute-start.19 = (bf16[4,9,16,512]{3,2,1,0:T(8,128)(2,1)S(1)}, bf16[4,9,16,512]{3,2,1,0:T(8,128)(2,1)S(1)}, u32[]{:S(2)}, u32[]{:S(2)}) collective-permute-start(bf16[4,9,16,512]{3,2,1,0:T(8,128)(2,1)S(1)} %dynamic-slice_bitcast_fusion.5), channel_id=1, source_target_pairs={{0,4},{2,6},{4,0},{6,2},{8,12},{10,14},{12,8},{14,10},{16,20},{18,... | collective-permute-start | bytes 1769480 | tf_op jit(solution)/shard_map/ppermute | solution.py:739
  348.2 24.2 %collective-permute-start.29 = (bf16[4,9,16,512]{3,2,1,0:T(8,128)(2,1)S(1)}, bf16[4,9,16,512]{3,2,1,0:T(8,128)(2,1)S(1)}, u32[]{:S(2)}, u32[]{:S(2)}) collective-permute-start(bf16[4,9,16,512]{3,2,1,0:T(8,128)(2,1)S(1)} %dynamic-slice_bitcast_fusion.4), channel_id=1, source_target_pairs={{0,4},{2,6},{4,0},{6,2},{8,12},{10,14},{12,8},{14,10},{16,20},{18,... | collective-permute-start | bytes 1769480 | tf_op jit(solution)/shard_map/ppermute | solution.py:739
  361.9 11.3 %collective-permute-start.20 = (bf16[2,9,16,512]{3,2,1,0:T(8,128)(2,1)S(1)}, bf16[2,9,16,512]{3,2,1,0:T(8,128)(2,1)S(1)}, u32[]{:S(2)}, u32[]{:S(2)}) collective-permute-start(bf16[2,9,16,512]{3,2,1,0:T(8,128)(2,1)S(1)} %dynamic-slice_bitcast_fusion.17), channel_id=1, source_target_pairs={{0,8},{2,10},{4,12},{6,14},{8,0},{10,2},{12,4},{14,6},{16,24},{18,... | collective-permute-start | bytes 884744 | tf_op jit(solution)/shard_map/ppermute | solution.py:739
  383.2 12.4 %collective-permute-start.31 = (bf16[1,9,16,512]{3,2,1,0:T(8,128)(2,1)S(1)}, bf16[1,9,16,512]{3,2,1,0:T(8,128)(2,1)S(1)}, u32[]{:S(2)}, u32[]{:S(2)}) collective-permute-start(bf16[1,9,16,512]{3,2,1,0:T(8,128)(2,1)S(1)} %constant_dynamic-slice_fusion.4), channel_id=1, source_target_pairs={{0,16},{2,18},{4,20},{6,22},{8,24},{10,26},{12,28},{14,30},{16,0},... | collective-permute-start | bytes 442376 | tf_op jit(solution)/shard_map/ppermute | solution.py:739
  383.3 17.7 %collective-permute-start.22 = (bf16[1,9,16,512]{3,2,1,0:T(8,128)(2,1)S(1)}, bf16[1,9,16,512]{3,2,1,0:T(8,128)(2,1)S(1)}, u32[]{:S(2)}, u32[]{:S(2)}) collective-permute-start(bf16[1,9,16,512]{3,2,1,0:T(8,128)(2,1)S(1)} %add_convert_fusion.2), channel_id=1, source_target_pairs={{0,16},{2,18},{4,20},{6,22},{8,24},{10,26},{12,28},{14,30},{16,0},... | collective-permute-start | bytes 442376 | tf_op jit(solution)/shard_map/ppermute | solution.py:739
  406.2 14.5 %collective-permute-start.33 = (bf16[2,9,16,512]{3,2,1,0:T(8,128)(2,1)S(1)}, bf16[2,9,16,512]{3,2,1,0:T(8,128)(2,1)S(1)}, u32[]{:S(2)}, u32[]{:S(2)}) collective-permute-start(bf16[2,9,16,512]{3,2,1,0:T(8,128)(2,1)S(1)} %maximum_select_fusion.11), channel_id=1, source_target_pairs={{0,8},{2,10},{4,12},{6,14},{8,0},{10,2},{12,4},{14,6},{16,24},{18,... | collective-permute-start | bytes 884744 | tf_op jit(solution)/shard_map/ppermute | solution.py:739
  420.7 16.3 %collective-permute-start.24 = (bf16[4,9,16,512]{3,2,1,0:T(8,128)(2,1)S(1)}, bf16[4,9,16,512]{3,2,1,0:T(8,128)(2,1)S(1)}, u32[]{:S(2)}, u32[]{:S(2)}) collective-permute-start(bf16[4,9,16,512]{3,2,1,0:T(8,128)(2,1)S(1)} %maximum_select_fusion.7), channel_id=1, source_target_pairs={{0,4},{2,6},{4,0},{6,2},{8,12},{10,14},{12,8},{14,10},{16,20},{18,... | collective-permute-start | bytes 1769480 | tf_op jit(solution)/shard_map/ppermute | solution.py:739
  422.4 27.2 %collective-permute-start.34 = (bf16[4,9,16,512]{3,2,1,0:T(8,128)(2,1)S(1)}, bf16[4,9,16,512]{3,2,1,0:T(8,128)(2,1)S(1)}, u32[]{:S(2)}, u32[]{:S(2)}) collective-permute-start(bf16[4,9,16,512]{3,2,1,0:T(8,128)(2,1)S(1)} %maximum_select_fusion.8), channel_id=1, source_target_pairs={{0,4},{2,6},{4,0},{6,2},{8,12},{10,14},{12,8},{14,10},{16,20},{18,... | collective-permute-start | bytes 1769480 | tf_op jit(solution)/shard_map/ppermute | solution.py:739
  432.7 17.1 %collective-permute-start.48 = (f32[32,1024]{1,0:T(8,128)S(1)}, f32[32,1024]{1,0:T(8,128)S(1)}, u32[]{:S(2)}, u32[]{:S(2)}) collective-permute-start(f32[32,1024]{1,0:T(8,128)S(1)} %convolution_bitcast_fusion), channel_id=1, source_target_pairs={{0,1},{1,0},{2,3},{3,2},{4,5},{5,4},{6,7},{7,6},{8,9},{9,8},{10,11... | collective-permute-start | bytes 393224 | tf_op jit(solution)/shard_map/ppermute | solution.py:736
  437.0 17.4 %collective-permute-start.56 = (bf16[4,4,16,512]{3,2,0,1:T(8,128)(2,1)S(1)}, bf16[4,4,16,512]{3,2,0,1:T(8,128)(2,1)S(1)}, u32[]{:S(2)}, u32[]{:S(2)}) collective-permute-start(bf16[4,4,16,512]{3,2,0,1:T(8,128)(2,1)S(1)} %maximum_select_fusion.12), channel_id=1, source_target_pairs={{0,4},{2,6},{4,0},{6,2},{8,12},{10,14},{12,8},{14,10},{16,20},{18,... | collective-permute-start | bytes 786440 | tf_op jit(solution)/shard_map/ppermute | solution.py:739
  (48 other events, 341.7 us)

commit v2 on v1

--- a/solution.py
+++ b/solution.py
@@ -396,6 +396,7 @@
 
 
 PIX = 1024
+BLOCK = 128
 BF = jnp.bfloat16
 F32 = jnp.float32
 NN = (((1,), (0,)), ((), ()))
@@ -459,19 +460,15 @@
 
 
 def taps_of(dest, masks, source, offset, depth, base, sign):
-    def step(index, carry):
-        piece = source[rows(index * 16, 16), :].astype(F32)
-        put_taps(dest, masks, piece, offset + index * 16, depth, base, sign)
-        return carry
-
-    lax.fori_loop(0, source.shape[0] // 16, step, 0, unroll=2)
-
-
-def place_conv(full, index, own, part, peer):
-    half, core = index[0], index[1]
+    for start in range(0, source.shape[0], 128):
+        piece = source[start : start + 128, :].astype(F32)
+        put_taps(dest, masks, piece, offset + start, depth, base, sign)
+
+
+def place_conv(full, index, own, peer):
+    half = index[0]
     full[:, rows(half * 256, 256), :] = own[...]
-    full[:, rows((1 - half) * 256 + core * 128, 128), :] = part[...]
-    full[:, rows((1 - half) * 256 + (1 - core) * 128, 128), :] = peer[...]
+    full[:, rows((1 - half) * 256, 256), :] = peer[...]
 
 
 def conv_dots(dest, full, col, dims, finish):
@@ -483,16 +480,23 @@
         dest[:, column : column + 512] = finish(total, column)
 
 
-def group_stats(block):
-    centre = jnp.mean(block, keepdims=True)
-    moved_block = block - centre
-    inverse = lax.rsqrt(jnp.mean(jnp.square(moved_block), keepdims=True) + EPS)
-    return centre, inverse, moved_block * inverse
-
-
-def keep_stats(stats, where, centre, inverse):
-    stats[where, 0:1] = jnp.broadcast_to(centre, (16, 1))
-    stats[where, 1:2] = jnp.broadcast_to(inverse, (16, 1))
+def grouped(block):
+    return block.reshape((-1, 16) + block.shape[1:])
+
+
+def group_mean(block):
+    return jnp.sum(block, axis=(1, 2), keepdims=True) * (1.0 / (16 * PIX))
+
+
+def group_stats(block, stats, where):
+    parts = grouped(block)
+    centre = group_mean(parts)
+    parts = parts - centre
+    inverse = lax.rsqrt(group_mean(jnp.square(parts)) + EPS)
+    count = block.shape[0]
+    stats[where, 0:1] = jnp.broadcast_to(centre, (count // 16, 16, 1)).reshape(count, 1)
+    stats[where, 1:2] = jnp.broadcast_to(inverse, (count // 16, 16, 1)).reshape(count, 1)
+    return (parts * inverse).reshape(block.shape)
 
 
 def unit_of(block, stats, where):
@@ -500,62 +504,59 @@
 
 
 def unit_back(grad, unit, inverse):
-    mean_grad = jnp.mean(grad, keepdims=True)
-    mean_both = jnp.mean(grad * unit, keepdims=True)
-    return (grad - mean_grad - unit * mean_both) * inverse
+    parts, units = grouped(grad), grouped(unit)
+    result = parts - group_mean(parts) - units * group_mean(parts * units)
+    return result.reshape(grad.shape) * inverse
 
 
 def row_sum(block):
     return jnp.sum(block, axis=1, keepdims=True)
 
 
-def first_conv(index, own, peer, par, w_own, w_part, w_peer, first, hidden, stats0, stats1, second, col, full):
+def first_conv(index, own, peer, par, w_own, w_peer, first, hidden, stats0, stats1, second, col, full):
     half = index[0]
-    place_conv(full, index, w_own, w_part, w_peer)
+    place_conv(full, index, w_own, w_peer)
     masks = edge_masks(1)
     for source, base in ((own, half * 256), (peer, (1 - half) * 256)):
 
         def norm(group, carry, source=source, base=base):
-            where = rows(base + group * 16, 16)
-            centre, inverse, unit = group_stats(source[rows(group * 16, 16), :].astype(F32))
-            keep_stats(stats0, where, centre, inverse)
+            where = rows(base + group * BLOCK, BLOCK)
+            unit = group_stats(source[rows(group * BLOCK, BLOCK), :].astype(F32), stats0, where)
             low = jax.nn.silu(unit * par[where, GAIN : GAIN + 1] + par[where, BIAS : BIAS + 1]).astype(BF)
             first[where, :] = low
-            put_taps(col, masks, low.astype(F32), base + group * 16, 512, 0, 1)
+            put_taps(col, masks, low.astype(F32), base + group * BLOCK, 512, 0, 1)
             return carry
 
-        lax.fori_loop(0, 16, norm, 0, unroll=2)
+        lax.fori_loop(0, 256 // BLOCK, norm, 0)
     conv_dots(hidden, full, col, NN, lambda total, column: total + par[:, CONVB : CONVB + 1])
 
     def again(group, carry):
-        where = rows(group * 16, 16)
-        centre, inverse, unit = group_stats(hidden[where, :])
-        keep_stats(stats1, where, centre, inverse)
+        where = rows(group * BLOCK, BLOCK)
+        unit = group_stats(hidden[where, :], stats1, where)
         normed = unit * par[where, GAIN + 1 : GAIN + 2] + par[where, BIAS + 1 : BIAS + 2]
         pre = normed * (1.0 + par[where, SCALE : SCALE + 1]) + par[where, SHIFT : SHIFT + 1]
         second[where, :] = jax.nn.silu(pre).astype(BF)
         return carry
 
-    lax.fori_loop(0, 32, again, 0, unroll=2)
-
-
-def second_conv(index, source, own, peer, par, w_own, w_part, w_peer, resid, stats2, normed, col, full):
+    lax.fori_loop(0, 512 // BLOCK, again, 0)
+
+
+def second_conv(index, source, own, peer, par, w_own, w_peer, resid, stats2, normed, col, full):
     half = index[0]
-    place_conv(full, index, w_own, w_part, w_peer)
+    place_conv(full, index, w_own, w_peer)
     taps_of(col, edge_masks(1), source, 0, 512, 0, 1)
     conv_dots(resid, full, col, NN, lambda total, column: total + par[:, CONVB + 1 : CONVB + 2])
     for picture, base in ((own, half * 256), (peer, (1 - half) * 256)):
 
         def norm(group, carry, picture=picture, base=base):
-            where = rows(base + group * 16, 16)
-            block = resid[where, :] + picture[rows(group * 16, 16), :].astype(F32)
+            where = rows(base + group * BLOCK, BLOCK)
+            block = resid[where, :] + picture[rows(group * BLOCK, BLOCK), :].astype(F32)
             resid[where, :] = block
-            centre, inverse, unit = group_stats(block)
-            keep_stats(stats2, where, centre, inverse)
+            unit = group_stats(block, stats2, where)
             normed[where, :] = (unit * par[where, GAIN + 2 : GAIN + 3] + par[where, BIAS + 2 : BIAS + 3]).astype(BF)
             return carry
 
-        lax.fori_loop(0, 16, norm, 0, unroll=2)
+        lax.fori_loop(0, 256 // BLOCK, norm, 0)
 
 
 def place_square(full, index, own, peer):
@@ -611,7 +612,7 @@
         )
 
     def back(group, carry):
-        where = rows(group * 16, 16)
+        where = rows(group * BLOCK, BLOCK)
         unit = unit_of(resid[where, :], stats2, where)
         grad = grad_normed[where, :]
         outer = grad_out[where, :].astype(F32)
@@ -625,7 +626,7 @@
         small[where, 3:4] = row_sum(outer)
         return carry
 
-    lax.fori_loop(0, 32, back, 0, unroll=2)
+    lax.fori_loop(0, 512 // BLOCK, back, 0)
 
 
 def projections(
@@ -646,14 +647,14 @@
 
 
 def second_back(
-    index, grad_branch, hidden, stats1, par, w_own, w_part, w_peer, grad_hidden, small, col, full, grad_second
+    index, grad_branch, hidden, stats1, par, w_own, w_peer, grad_hidden, small, col, full, grad_second
 ):
-    place_conv(full, index, w_own, w_part, w_peer)
+    place_conv(full, index, w_own, w_peer)
     taps_of(col, edge_masks(-1), grad_branch, 0, 512, 0, -1)
     conv_dots(grad_second, full, col, TN, lambda total, column: total)
 
     def back(group, carry):
-        where = rows(group * 16, 16)
+        where = rows(group * BLOCK, BLOCK)
         unit = unit_of(hidden[where, :], stats1, where)
         gain = par[where, GAIN + 1 : GAIN + 2]
         normed = unit * gain + par[where, BIAS + 1 : BIAS + 2]
@@ -669,22 +670,22 @@
         small[where, 4:5] = row_sum(low.astype(F32))
         return carry
 
-    lax.fori_loop(0, 32, back, 0, unroll=2)
+    lax.fori_loop(0, 512 // BLOCK, back, 0)
 
 
 def first_back(
-    index, grad_hidden, own, peer, stats0, par, grad_resid, w_own, w_part, w_peer,
+    index, grad_hidden, own, peer, stats0, par, grad_resid, w_own, w_peer,
     near, far, small, col, full, grad_first,
 ):
     half = index[0]
-    place_conv(full, index, w_own, w_part, w_peer)
+    place_conv(full, index, w_own, w_peer)
     taps_of(col, edge_masks(-1), grad_hidden, 0, 512, 0, -1)
     conv_dots(grad_first, full, col, TN, lambda total, column: total)
     for picture, base, dest in ((own, half * 256, near), (peer, (1 - half) * 256, far)):
 
         def back(group, carry, picture=picture, base=base, dest=dest):
-            here = rows(group * 16, 16)
-            where = rows(base + group * 16, 16)
+            here = rows(group * BLOCK, BLOCK)
+            where = rows(base + group * BLOCK, BLOCK)
             unit = unit_of(picture[here, :].astype(F32), stats0, where)
             gain = par[where, GAIN : GAIN + 1]
             grad = grad_first[where, :] * silu_slope(unit * gain + par[where, BIAS : BIAS + 1])
@@ -694,7 +695,7 @@
             small[where, 1:2] = row_sum(grad)
             return carry
 
-        lax.fori_loop(0, 16, back, 0, unroll=2)
+        lax.fori_loop(0, 256 // BLOCK, back, 0)
 
 
 def weight_back(index, grad_own, grad_peer, source_own, source_peer, grads, col, turned):
@@ -707,6 +708,337 @@
         result = mm(col[tap * 256 : (tap + 1) * 256, :], turned[...]).astype(BF)
         for part in range(16):
             grads[part, tap] = result[part * 16 : (part + 1) * 16]
+
+
+def remote(source, dest, sends, recvs, slot, target):
+    return pltpu.make_async_remote_copy(
+        src_ref=source,
+        dst_ref=dest,
+        send_sem=sends.at[slot],
+        recv_sem=recvs.at[slot],
+        device_id=target,
+        device_id_type=pl.DeviceIdType.MESH,
+    )
+
+
+def meet(targets):
+    barrier = pltpu.get_barrier_semaphore()
+    for target in targets:
+        pl.semaphore_signal(barrier, inc=1, device_id=target, device_id_type=pl.DeviceIdType.MESH)
+    pl.semaphore_wait(barrier, len(targets))
+
+
+def position():
+    place = lax.axis_index("batch")
+    return place, place % 2, (place // 2) % 2, place // 4
+
+
+PIECES = 6
+KINDS = 10
+
+
+def gather(
+    pre_embed, params, emb_weight, emb_bias, images, conv_weight, qkv_weight, proj_weight,
+    par, image_peer, conv_peer, qkv_peer, proj_peer,
+    par_send, par_recv, sends, recvs, few_sends, few_recvs,
+):
+    half = lax.axis_index("head")
+    place, core, up, deep = position()
+    z_low = deep % 2
+    to_x = {"head": 1 - half}
+    to_y = {"batch": place + 2 * (1 - 2 * up)}
+    to_z = {"batch": place + 4 * (1 - 2 * z_low)}
+    to_core = {"batch": place + (1 - 2 * core)}
+    meet([to_x, to_y, to_z, to_core])
+
+    def block(flip_core=0, flip_y=0, flip_z=0):
+        c = 1 - core if flip_core else core
+        y = 1 - up if flip_y else up
+        z = 1 - z_low if flip_z else z_low
+        return (c + 2 * y + 4 * z) * 32
+
+    def views(piece, near, start, count):
+        where = rows(start, count)
+        if piece < 4:
+            taps = pl.ds(0, 5) if piece % 2 == 0 else pl.ds(5, 4)
+            return (conv_weight if near else conv_peer).at[piece // 2, taps, where, :]
+        if piece == 4:
+            return (qkv_weight if near else qkv_peer).at[:, where, :]
+        return (proj_weight if near else proj_peer).at[where, :]
+
+    def copy(piece, kind, start, count, target, near=False):
+        return remote(
+            views(piece, near, start, count), views(piece, False, start, count),
+            sends.at[piece], recvs.at[piece], kind, target,
+        )
+
+    def regions(flip_core):
+        return (
+            (block(flip_core), 32),
+            (block(flip_core, 1), 32),
+            (block(flip_core, 0, 1), 32),
+            (block(flip_core, 1, 1), 16),
+            (block(flip_core, 1, 1) + 16, 16),
+        )
+
+    mine, others = regions(0), regions(1)
+
+    def arrived(piece, kind):
+        start, count = mine[kind] if kind < 5 else others[kind - 5]
+        copy(piece, kind, start, count, to_core).wait_recv()
+
+    def over_x(piece):
+        arrived(piece, 0)
+        for kind, target in ((1, to_y), (2, to_z), (5, to_core)):
+            copy(piece, kind, block(), 32, target).start()
+
+    def over_yz(piece):
+        arrived(piece, 2)
+        copy(piece, 3, block(0, 0, 1), 16, to_y).start()
+        copy(piece, 7, block(0, 0, 1), 32, to_core).start()
+        arrived(piece, 1)
+        copy(piece, 4, block(0, 1, 0) + 16, 16, to_z).start()
+        copy(piece, 6, block(0, 1, 0), 32, to_core).start()
+
+    def diagonal(piece):
+        arrived(piece, 3)
+        copy(piece, 8, block(0, 1, 1), 16, to_core).start()
+        arrived(piece, 4)
+        copy(piece, 9, block(0, 1, 1) + 16, 16, to_core).start()
+
+    for piece in range(PIECES):
+        copy(piece, 0, block(), 32, to_x, near=True).start()
+    picture = remote(images.at[1 - half], image_peer, few_sends, few_recvs, 0, to_x)
+    picture.start()
+    embed = jax.nn.silu(pre_embed[...])
+    own_row = jnp.where(half == 0, embed[0:1], embed[1:2])
+    peer_row = jnp.where(half == 0, embed[1:2], embed[0:1])
+    near = rows(half * 256, 256)
+    par[near, 0:9] = params[...]
+    par_send[:, 0:9] = params[...]
+    for which in range(2):
+        dense = emb_weight[which].astype(F32)
+        offset = emb_bias[:, which : which + 1]
+        par[near, SCALE + which : SCALE + which + 1] = row_sum(dense * own_row) + offset
+        par_send[:, SCALE + which : SCALE + which + 1] = row_sum(dense * peer_row) + offset
+    block_copy = remote(par_send, par_recv, few_sends, few_recvs, 1, to_x)
+    block_copy.start()
+
+    over_x(0)
+    over_x(1)
+    over_yz(0)
+    over_x(2)
+    over_yz(1)
+    diagonal(0)
+    over_x(3)
+    over_yz(2)
+    diagonal(1)
+    over_x(4)
+    over_x(5)
+    over_yz(3)
+    diagonal(2)
+    over_yz(4)
+    over_yz(5)
+    diagonal(3)
+    diagonal(4)
+    diagonal(5)
+    block_copy.wait_recv()
+    par[rows((1 - half) * 256, 256), :] = par_recv[:, 0:11]
+    picture.wait_recv()
+    for piece in range(PIECES):
+        for kind in range(5, 10):
+            arrived(piece, kind)
+    for piece in range(PIECES):
+        copy(piece, 0, block(), 32, to_x).wait_send()
+        for kind, start, count in (
+            (1, block(), 32), (2, block(), 32), (5, block(), 32),
+            (3, block(0, 0, 1), 16), (7, block(0, 0, 1), 32),
+            (4, block(0, 1, 0) + 16, 16), (6, block(0, 1, 0), 32),
+            (8, block(0, 1, 1), 16), (9, block(0, 1, 1) + 16, 16),
+        ):
+            copy(piece, kind, start, count, to_x).wait_send()
+    picture.wait_send()
+    block_copy.wait_send()
+
+
+def gather_call(pre_embed, params, emb_weight, emb_bias, images, conv_weight, qkv_weight, proj_weight):
+    anywhere = pl.BlockSpec(memory_space=pl.ANY)
+    return pl.pallas_call(
+        gather,
+        out_shape=[
+            out((512, 11), F32),
+            out(images.shape[1:], BF),
+            out(conv_weight.shape, BF),
+            out(qkv_weight.shape, BF),
+            out(proj_weight.shape, BF),
+        ],
+        in_specs=[VMEM] * 4 + [anywhere] * 4,
+        out_specs=[VMEM] + [anywhere] * 4,
+        scratch_shapes=[
+            pltpu.VMEM((256, 128), F32),
+            pltpu.VMEM((256, 128), F32),
+            pltpu.SemaphoreType.DMA((PIECES, KINDS)),
+            pltpu.SemaphoreType.DMA((PIECES, KINDS)),
+            pltpu.SemaphoreType.DMA((2,)),
+            pltpu.SemaphoreType.DMA((2,)),
+        ],
+        cost_estimate=pl.CostEstimate(flops=0, bytes_accessed=100 * 2**20, transcendentals=0),
+        compiler_params=pltpu.CompilerParams(
+            collective_id=1, has_side_effects=True, vmem_limit_bytes=24 * 2**20
+        ),
+    )(pre_embed, params, emb_weight, emb_bias, images, conv_weight, qkv_weight, proj_weight)
+
+
+SENDS = 11
+
+
+class Sum:
+    def __init__(self, source, total, scratch, planes):
+        self.source, self.total, self.planes = source, total, planes
+        self.sends, self.recvs, self.core_in, self.first, self.y_in, self.second, self.z_in = scratch[:7]
+        if planes:
+            self.x_in, self.middle = scratch[7:]
+        self.half = lax.axis_index("head")
+        self.place, self.core, self.up, self.deep = position()
+        self.steps = [self.start, self.core_done]
+        if planes:
+            self.steps.append(self.x_done)
+        self.steps += [self.y_done, self.z_done, self.z_back, self.y_back, self.finish]
+        self.open = []
+
+    def to_core(self):
+        return {"batch": self.place + 1 - 2 * self.core}
+
+    def to_y(self):
+        return {"batch": self.place + 2 * (1 - 2 * self.up)}
+
+    def to_z(self, ahead):
+        return {"batch": (self.deep + ahead) % 4 * 4 + self.place % 4}
+
+    def send(self, slot, source, dest, target):
+        copy = remote(source, dest, self.sends, self.recvs, slot, target)
+        copy.start()
+        self.open.append(copy)
+
+    def arrived(self, slot, dest):
+        remote(dest, dest, self.sends, self.recvs, slot, self.to_core()).wait_recv()
+
+    def start(self):
+        other = 1 - self.core
+        part = self.source.at[other] if self.planes else self.source.at[pl.ds(other * 8, 8)]
+        self.send(0, part, self.core_in, self.to_core())
+
+    def add(self, dest, left, *right):
+        total = left.astype(F32)
+        for term in right:
+            total = total + term.astype(F32)
+        dest[...] = total.astype(BF)
+
+    def core_done(self):
+        self.arrived(0, self.core_in)
+        if self.planes:
+            self.add(self.middle, self.source[self.core], self.core_in[...])
+            self.send(10, self.middle.at[1 - self.half], self.x_in, {"head": 1 - self.half})
+        else:
+            self.add(self.first, self.source[pl.ds(self.core * 8, 8)], self.core_in[...])
+            self.send_y()
+
+    def x_done(self):
+        self.arrived(10, self.x_in)
+        self.add(self.first, self.middle[self.half], self.x_in[...])
+        self.send_y()
+
+    def send_y(self):
+        self.send(1, self.first.at[pl.ds((1 - self.up) * 4, 4)], self.y_in, self.to_y())
+
+    def y_done(self):
+        self.arrived(1, self.y_in)
+        self.add(self.second, self.first[pl.ds(self.up * 4, 4)], self.y_in[...])
+        for ahead in (2, 1, 3):
+            chunk = self.second.at[(self.deep + ahead) % 4]
+            self.send(1 + ahead, chunk, self.z_in.at[ahead - 1], self.to_z(ahead))
+
+    def chunk(self, deep):
+        return self.core * 8 + self.up * 4 + deep
+
+    def z_done(self):
+        for ahead in (1, 2, 3):
+            self.arrived(1 + ahead, self.z_in.at[ahead - 1])
+        mine = self.total.at[self.chunk(self.deep)]
+        self.add(mine, self.second[self.deep], self.z_in[0], self.z_in[1], self.z_in[2])
+        for ahead in (2, 1, 3):
+            self.send(4 + ahead, mine, mine, self.to_z(ahead))
+
+    def z_back(self):
+        for ahead in (1, 2, 3):
+            self.arrived(4 + ahead, self.total.at[self.chunk((self.deep + 4 - ahead) % 4)])
+        part = self.total.at[pl.ds(self.chunk(0), 4)]
+        self.send(8, part, part, self.to_y())
+
+    def y_back(self):
+        self.arrived(8, self.total.at[pl.ds(self.core * 8 + (1 - self.up) * 4, 4)])
+        part = self.total.at[pl.ds(self.core * 8, 8)]
+        self.send(9, part, part, self.to_core())
+
+    def finish(self):
+        self.arrived(9, self.total.at[pl.ds((1 - self.core) * 8, 8)])
+        for copy in self.open:
+            copy.wait_send()
+
+
+def sum_scratch(tail, planes):
+    shapes = [
+        pltpu.SemaphoreType.DMA((SENDS,)),
+        pltpu.SemaphoreType.DMA((SENDS,)),
+        pltpu.VMEM(((2, 8) if planes else (8,)) + tail, BF),
+        pltpu.VMEM((8,) + tail, BF),
+        pltpu.VMEM((4,) + tail, BF),
+        pltpu.VMEM((4,) + tail, BF),
+        pltpu.VMEM((3,) + tail, BF),
+    ]
+    if planes:
+        shapes += [pltpu.VMEM((8,) + tail, BF), pltpu.VMEM((2, 8) + tail, BF)]
+    return shapes
+
+
+def batch_sums(squares, grads1, grads0, squares_sum, sum1, sum0, *scratch):
+    place, core, up, deep = position()
+    half = lax.axis_index("head")
+    targets = [{"head": 1 - half}, {"batch": place + 1 - 2 * core}, {"batch": place + 2 * (1 - 2 * up)}]
+    targets += [{"batch": (deep + ahead) % 4 * 4 + place % 4} for ahead in (1, 2, 3)]
+    meet(targets)
+    chains = [Sum(squares, squares_sum, scratch[:9], True)]
+    scratch = scratch[9:]
+    for source, total in ((grads1, sum1), (grads0, sum0)):
+        for number, taps in enumerate(TAP_PARTS):
+            chains.append(
+                Sum(source.at[:, taps], total.at[:, taps], scratch[:7], False)
+            )
+            scratch = scratch[7:]
+    for tick in range(len(chains) + 8):
+        for number, chain in enumerate(chains):
+            if 0 <= tick - number < len(chain.steps):
+                chain.steps[tick - number]()
+
+
+TAP_PARTS = (slice(0, 3), slice(3, 6), slice(6, 9))
+
+
+def batch_sums_call(squares, grads1, grads0):
+    scratch = sum_scratch((4, 16, 512), True)
+    for part in TAP_PARTS * 2:
+        scratch += sum_scratch((part.stop - part.start, 16, 512), False)
+    return pl.pallas_call(
+        batch_sums,
+        out_shape=[out((16, 4, 16, 512), BF), out(grads1.shape, BF), out(grads0.shape, BF)],
+        in_specs=[VMEM] * 3,
+        out_specs=[VMEM] * 3,
+        scratch_shapes=scratch,
+        cost_estimate=pl.CostEstimate(flops=0, bytes_accessed=200 * 2**20, transcendentals=0),
+        compiler_params=pltpu.CompilerParams(
+            collective_id=2, has_side_effects=True, vmem_limit_bytes=56 * 2**20
+        ),
+    )(squares, grads1, grads0)
 
 
 def paired(
@@ -729,7 +1061,6 @@
 ):
     half = lax.axis_index("head")
     place = lax.axis_index("batch")
-    core = place % 2
     bits = batch_size.bit_length() - 1
 
     def across(value):
@@ -757,39 +1088,22 @@
             my_bit(bit) == 0, jnp.concatenate([value, peer]), jnp.concatenate([peer, value])
         )
 
-    def halve(value, bit):
-        pair = value.reshape((2, value.shape[0] // 2) + value.shape[1:])
-        arrived = over(pick(pair, 1 - my_bit(bit)), bit)
-        return (pick(pair, my_bit(bit)).astype(F32) + arrived.astype(F32)).astype(BF)
-
     image_own = pick(images, half)
-    image_peer = across(pick(images, 1 - half))
     cot_own = pick(cotangent, half)
     cot_peer = across(pick(cotangent, 1 - half))
-
-    def conv_parts(which):
-        own = conv_weight[which]
-        part = across(lax.dynamic_slice_in_dim(own, core * 128, 128, 1))
-        return own, part, over(part, 0)
-
-    weights0 = conv_parts(0)
-    weights1 = conv_parts(1)
-    q_peer = across(qkv_weight)
-    p_peer = across(proj_weight)
 
     table_rows = jnp.stack([pick(class_table, classes[slot]) for slot in range(2)]).astype(F32)
     emb_width = class_table.shape[1]
     pre_embed = jnp.stack([features(timesteps[slot], emb_width) for slot in range(2)]) + table_rows
-    embed = jax.nn.silu(pre_embed)
+    params = jnp.concatenate([norm_gain, norm_bias, conv_bias, proj_bias[None]]).T
+    par, image_peer, conv_peer, q_peer, p_peer = gather_call(
+        pre_embed, params, emb_weight, emb_bias.T, images, conv_weight, qkv_weight, proj_weight
+    )
+    weights0 = (conv_weight[0], conv_peer[0])
+    weights1 = (conv_weight[1], conv_peer[1])
     dense = emb_weight.astype(F32)
-    mod = jnp.einsum("mce,be->bmc", dense, embed, precision=HIGH) + emb_bias[None]
-    params = jnp.concatenate([norm_gain, norm_bias, conv_bias, proj_bias[None]])
-    par_near = jnp.concatenate([params, pick(mod, half)])
-    par_far = across(jnp.concatenate([params, pick(mod, 1 - half)]))
-    par = by_half(par_near, par_far, 1).T
-
     live = (half < live_count[0]).astype(jnp.int32)
-    scalars = jnp.stack([half, core, live]).astype(jnp.int32)
+    scalars = jnp.stack([half, 0 * half, live]).astype(jnp.int32)
     full_bf = out((512, PIX), BF)
     full_f32 = out((512, PIX), F32)
     half_bf = out((256, PIX), BF)
@@ -854,25 +1168,14 @@
     )
     far = across(far).astype(F32)
 
-    def reduce_conv(value):
-        for bit in range(bits):
-            value = halve(value, bit)
-        for bit in reversed(range(bits)):
-            value = widen(value, bit)
-        return value.transpose(1, 0, 2, 3).reshape(9, 256, 512).astype(F32)
-
-    conv_total1 = reduce_conv(conv_grad1)
-    conv_total0 = reduce_conv(conv_grad0)
-
-    squares = halve(square_grads, 0)[0]
-    keep_part, send_part = pick(squares, half), pick(squares, 1 - half)
-    squares = (keep_part.astype(F32) + across(send_part).astype(F32)).astype(BF)
-    for bit in range(1, bits):
-        squares = halve(squares, bit)
-    for bit in reversed(range(bits)):
-        squares = widen(squares, bit)
-    squares = squares.transpose(1, 0, 2, 3).reshape(4, 256, 512).astype(F32)
-
+    square_sum, conv_sum1, conv_sum0 = batch_sums_call(
+        square_grads.reshape(2, 2, 8, 4, 16, 512), conv_grad1, conv_grad0
+    )
+
+    def whole(value):
+        return value.transpose(1, 0, 2, 3).reshape(value.shape[1], 256, 512).astype(F32)
+
+    conv_total1, conv_total0, squares = whole(conv_sum1), whole(conv_sum0), whole(square_sum)
     small = jnp.concatenate([small0, small1, small2], 1).T.reshape(11, 2, 256).transpose(1, 0, 2)
     small_own, small_peer = pick(small, half), across(pick(small, 1 - half))
     sums = small_own + small_peer
@@ -941,6 +1244,6 @@
     )
     body = shards
     batch_size = mesh.shape["batch"]
-    if mesh.shape["head"] == 2 and batch_size in (8, 16):
+    if mesh.shape["head"] == 2 and batch_size == 16:
         body = functools.partial(paired, batch_size)
     return jax.shard_map(body, mesh=mesh, in_specs=in_specs, out_specs=out_specs, check_vma=False)

time: 470 us -> 385 us (0.82)
  waiting for transfers between devices: 168 us -> 25.2 us
  Pallas kernels: 178 us -> 272 us
  starting transfers between devices: 56.1 us -> 26.3 us
    pallas_call x0 -> x2, Pallas kernels: none -> 142 us  [the longest x1 107 us: batch_sums_call(): pl.pallas_call(batch_sums, out_shape=[out((16, 4, 16, 512), BF), out(grad...]
    ppermute x42 -> x16, waiting for transfers between devices: 106 us -> 17.2 us  [over(): lax.ppermute(value, 'batch', [(i, i ^ 1 << bit) for i in range(batch_size)])]
    ppermute x16 -> x9, waiting for transfers between devices: 62.1 us -> 7.98 us  [across(): return lax.ppermute(value, 'head', [(0, 1), (1, 0)])]
    pallas_call x8, Pallas kernels: 178 us -> 129 us  [kernel_call(): pl.pallas_call(kernel, out_shape=outs, in_specs=[SMEM] + [VMEM] * len(arg...]
    ppermute x42 -> x16, starting transfers between devices: 36.3 us -> 13.7 us  [over(): lax.ppermute(value, 'batch', [(i, i ^ 1 << bit) for i in range(batch_size)])]
    squeeze x0 -> x2, local copies, waits for them, and re-layouts: none -> 8.17 us  [paired(): weights1 = (conv_weight[1], conv_peer[1])]
    ppermute x16 -> x9, starting transfers between devices: 19.8 us -> 12.6 us  [across(): return lax.ppermute(value, 'head', [(0, 1), (1, 0)])]
    slice x1 -> x0, local copies, waits for them, and re-layouts: 5.94 us -> none  [conv_parts(): own = conv_weight[which]]
  transfers between devices with their start and end apart: 58 -> 25, of which waited for: 29 -> 11; matrix products, arithmetic and copies ran while one was open for 9% -> 10% of each run, Pallas kernels for 38% -> 72%
where the time goes in v2:
time: 385 us; the launch traced here: 379 us
  Pallas kernels  272 us (71%)
  local copies, waits for them, and re-layouts  29.4 us (8%)
  starting transfers between devices  26.3 us (7%)
  waiting for transfers between devices  25.2 us (7%)
  other arithmetic  12.3 us (3%)
  matrix products  7.52 us (2%)
  between operations  7.12 us (2%)
    pallas_call x8, Pallas kernels, kernel_call(): pl.pallas_call(kernel, out_shape=outs, in_specs=[SMEM] + [VMEM] * len(arg...  129 us
    pallas_call x1, Pallas kernels, batch_sums_call(): pl.pallas_call(batch_sums, out_shape=[out((16, 4, 16, 512), BF), out(grad...  107 us
    pallas_call x1, Pallas kernels, gather_call(): pl.pallas_call(gather, out_shape=[out((512, 11), F32), out(images.shape[1...  35.4 us
    ppermute x16, waiting for transfers between devices, over(): lax.ppermute(value, 'batch', [(i, i ^ 1 << bit) for i in range(batch_size)])  17.2 us
    ppermute x16, starting transfers between devices, over(): lax.ppermute(value, 'batch', [(i, i ^ 1 << bit) for i in range(batch_size)])  13.7 us
    ppermute x9, starting transfers between devices, across(): return lax.ppermute(value, 'head', [(0, 1), (1, 0)])  12.6 us
    squeeze x2, local copies, waits for them, and re-layouts, paired(): weights1 = (conv_weight[1], conv_peer[1])  8.17 us
    ppermute x9, waiting for transfers between devices, across(): return lax.ppermute(value, 'head', [(0, 1), (1, 0)])  7.98 us
  transfers between devices with their start and end apart: 25, of which 11 were waited for; matrix products, arithmetic and copies ran while one was open for 10% of the time, Pallas kernels for 72%

profile of v2, /device:TPU:0, one launch (start us, length us, event | category | flops | bytes accessed | tf_op | source)
XLA Modules:
  0.0 379.4 jit_solution(13258507957105974128)
XLA Ops:
  0.7 2.4 dynamic-slice_bitcast_fusion.5
  3.1 2.9 collective-permute-start
  17.2 5.6 %slice_bitcast_fusion.1 = (bf16[9,256,512]{2,1,0:T(8,128)(2,1)}, bf16[9,256,512]{2,1,0:T(8,128)(2,1)}) fusion(bf16[2,9,256,512]{3,2,1,0:T(8,128)(2,1)} %conv_weight.1), kind=kLoop, calls=%fused_computation.2 | loop fusion | bytes 9437184 | tf_op jit(solution)/shard_map/squeeze | solution.py:1103
  22.8 35.4 %shard_map.238 = (f32[512,11]{1,0:T(8,128)S(1)}, bf16[256,1024]{1,0:T(8,128)(2,1)S(1)}, bf16[2,9,256,512]{3,2,1,0:T(8,128)(2,1)S(1)}, bf16[3,256,512]{2,1,0:T(8,128)(2,1)S(1)}, bf16[256,512]{1,0:T(8,128)(2,1)S(1)}) custom-call(f32[2,1024]{1,0:T(2,128)S(1)} %maximum_add_fusion.pre_embed, f32[256,9]{1,0:T(8,128)S(1)} %bitcast.70, ...), custom_call_target="tpu_custom_call" | custom-call | bytes 104857600 | tf_op jit(solution)/shard_map/pallas_call | solution.py:866
  59.8 2.6 slice_bitcast_fusion
  63.6 16.3 %shard_map.239 = (bf16[512,1024]{1,0:T(8,128)(2,1)}, f32[512,1024]{1,0:T(8,128)}, f32[512,2]{1,0:T(8,128)}, f32[512,2]{1,0:T(8,128)}, bf16[512,1024]{1,0:T(8,128)(2,1)}) custom-call(s32[3]{0:T(128)} %pad_add_fusion.index, bf16[256,1024]{1,0:T(8,128)(2,1)} %dynamic-slice_bitcast_fusion.7.own, bf16[256,1024]{1,0:T(8,128)(2,1)} %copy-done.7, ...), custom_call_target="tpu_custom_call" | custom-call | flops 4831838208 | bytes 9992192 | tf_op jit(solution)/shard_map/pallas_call | solution.py:418
  80.1 1.9 collective-permute-start.9
  82.0 11.9 %shard_map.240 = (f32[512,1024]{1,0:T(8,128)}, f32[512,2]{1,0:T(8,128)}, bf16[512,1024]{1,0:T(8,128)(2,1)}) custom-call(s32[3]{0:T(128)} %pad_add_fusion.index, bf16[512,1024]{1,0:T(8,128)(2,1)} %get-tuple-element.46.source.source_own, bf16[256,1024]{1,0:T(8,128)(2,1)} %dynamic-slice_bitcast_fusion.7.own, bf16[256,1024]{1,0:T(8,128)(2,1)} %copy-done.7, ...), custom_call_target="tpu_custom_call" | custom-call | flops 4831838208 | bytes 9988096 | tf_op jit(solution)/shard_map/pallas_call | solution.py:418
  94.5 3.0 collective-permute-done.21
  97.9 1.8 collective-permute-start.17
  101.3 2.6 collective-permute-start.23
  105.8 2.1 collective-permute-done.18
  108.5 43.5 %shard_map.241 = (bf16[512,1024]{1,0:T(8,128)(2,1)}, bf16[512,1024]{1,0:T(8,128)(2,1)}, bf16[512,1024]{1,0:T(8,128)(2,1)}, bf16[512,1024]{1,0:T(8,128)(2,1)}, bf...) custom-call(s32[3]{0:T(128)} %pad_add_fusion.index, ...), custom_call_target="tpu_custom_call" | custom-call | flops 19327352832 | bytes 14714880 | tf_op jit(solution)/shard_map/pallas_call | solution.py:418
  152.0 14.9 %shard_map.243 = (bf16[512,1024]{1,0:T(8,128)(2,1)}, f32[512,5]{1,0:T(8,128)}) custom-call(s32[3]{0:T(128)} %pad_add_fusion.index, bf16[512,1024]{1,0:T(8,128)(2,1)} %get-tuple-element.58.grad_branch, f32[512,1024]{1,0:T(8,128)} %get-tuple-element.59.hidden, f32[512,2]{1,0:T(8,128)} %get-tuple-element.60.stats1, f32[512,11]{1,0:T(8,128)} %copy-done.4, ...), custom_call_target="tpu_custom_call" | custom-call | flops 4831838208 | bytes 8949760 | tf_op jit(solution)/shard_map/pallas_call | solution.py:418
  166.9 14.0 %shard_map.244 = (f32[256,1024]{1,0:T(8,128)}, bf16[256,1024]{1,0:T(8,128)(2,1)}, f32[512,2]{1,0:T(8,128)}) custom-call(s32[3]{0:T(128)} %pad_add_fusion.index, bf16[512,1024]{1,0:T(8,128)(2,1)} %get-tuple-element.61.grad_hidden, bf16[256,1024]{1,0:T(8,128)(2,1)} %dynamic-slice_bitcast_fusion.7.own, bf16[256,1024]{1,0:T(8,128)(2,1)} %copy-done.7, ...), custom_call_target="tpu_custom_call" | custom-call | flops 4831838208 | bytes 10516480 | tf_op jit(solution)/shard_map/pallas_call | solution.py:418
  182.4 1.8 collective-permute-start.3
  184.1 8.0 %shard_map.242 = (bf16[512,1024]{1,0:T(8,128)(2,1)}, bf16[2,2,8,4,16,512]{5,4,3,2,1,0:T(8,128)(2,1)}) custom-call(s32[3]{0:T(128)} %pad_add_fusion.index, bf16[512,1024]{1,0:T(8,128)(2,1)} %get-tuple-element.47.normed, f32[512,1024]{1,0:T(8,128)} %get-tuple-element.48.resid, f32[512,11]{1,0:T(8,128)} %copy-done.4, ...), custom_call_target="tpu_custom_call" | custom-call | flops 2415919104 | bytes 12081152 | tf_op jit(solution)/shard_map/pallas_call | solution.py:418
  195.6 1.8 collective-permute-start.5
  199.4 1.7 collective-permute-start.6
  201.2 1.9 collective-permute-done.6
  203.1 1.7 collective-permute-start.10
  206.1 3.9 %collective-permute-done.7 = f32[11,256]{1,0:T(8,128)S(1)} collective-permute-done((f32[11,256]{1,0:T(8,128)S(1)}, f32[11,256]{1,0:T(8,128)S(1)}, u32[]{:S(2)}, u32[]{:S(2)}) %collective-permute-start.7) | collective-permute-done | bytes 11296 | tf_op jit(solution)/shard_map/ppermute | solution.py:1070
  216.0 1.6 collective-permute-start.24
  217.6 3.2 fusion.2
  220.7 8.0 %collective-permute-done.24 = f32[32,1024]{1,0:T(8,128)S(1)} collective-permute-done((f32[32,1024]{1,0:T(8,128)S(1)}, f32[32,1024]{1,0:T(8,128)S(1)}, u32[]{:S(2)}, u32[]{:S(2)}) %collective-permute-start.24) | collective-permute-done | bytes 131104 | tf_op jit(solution)/shard_map/ppermute | solution.py:1067
  228.7 1.6 collective-permute-start.2
  230.3 3.8 fusion
  234.8 10.5 %shard_map.246.grads0 = bf16[16,9,16,512]{3,2,1,0:T(8,128)(2,1)} custom-call(s32[3]{0:T(128)} %pad_add_fusion.index, bf16[256,1024]{1,0:T(8,128)(2,1)} %get-tuple-element.81.grad_own, bf16[256,1024]{1,0:T(8,128)(2,1)} %copy-done.21, bf16[512,1024]{1,0:T(8,128)(2,1)} %get-tuple-element.70.source_own, bf16[512,1024]{1,0:T(8,128)(2,1)} %collective-permute-done.11.source_peer), custom_call_target="tpu_custom_call" | custom-call | flops 4831838208 | bytes 5505024 | tf_op jit(solution)/shard_map/pallas_call | solution.py:418
  246.5 10.2 %shard_map.245.grads1 = bf16[16,9,16,512]{3,2,1,0:T(8,128)(2,1)} custom-call(s32[3]{0:T(128)} %pad_add_fusion.index, bf16[256,1024]{1,0:T(8,128)(2,1)} %get-tuple-element.83.grad_own, bf16[256,1024]{1,0:T(8,128)(2,1)} %copy-done.22, bf16[512,1024]{1,0:T(8,128)(2,1)} %get-tuple-element.46.source.source_own, bf16[512,1024]{1,0:T(8,128)(2,1)} %copy-done.19), custom_call_target="tpu_custom_call" | custom-call | flops 4831838208 | bytes 5505024 | tf_op jit(solution)/shard_map/pallas_call | solution.py:418
  256.7 106.7 %shard_map.247 = (bf16[16,4,16,512]{3,2,1,0:T(8,128)(2,1)}, bf16[16,9,16,512]{3,2,1,0:T(8,128)(2,1)}, bf16[16,9,16,512]{3,2,1,0:T(8,128)(2,1)}) custom-call(bf16[2,2,8,4,16,512]{5,4,3,2,1,0:T(8,128)(2,1)} %get-tuple-element.69.squares, bf16[16,9,16,512]{3,2,1,0:T(8,128)(2,1)} %shard_map.245.grads1, bf16[16,9,16,512]{3,2,1,0:T(8,128)(2,1)} %shard_map.246.grads0), custom_call_target="tpu_custom_call" | custom-call | bytes 209715200 | tf_op jit(solution)/shard_map/pallas_call | solution.py:1031
  372.2 1.5 maximum_select_fusion
  373.7 4.4 %maximum_convert_fusion = f32[2,9,256,512]{3,2,1,0:T(8,128)} fusion(bf16[1,9,256,512]{3,2,1,0:T(8,128)(2,1)S(1)} %bitcast.73, bf16[1,9,256,512]{3,2,1,0:T(8,128)(2,1)S(1)} %bitcast.72), kind=kLoop, calls=%fused_computation | loop fusion | flops 4718592 | bytes 14155776 | tf_op jit(solution)/shard_map/stack | solution.py:1202
  (143 shorter events, 39.0 us)
Async XLA Ops:
  0.6 15.6 %copy-start.18 = (f32[2,256]{1,0:T(2,128)S(1)}, f32[2,256]{1,0:T(2,128)}, u32[]{:S(2)}) copy-start(f32[2,256]{1,0:T(2,128)} %param.24) | copy-start | bytes 6148
  0.7 15.7 %copy-start.1 = (bf16[2,256,1024]{2,1,0:T(8,128)(2,1)S(1)}, bf16[2,256,1024]{2,1,0:T(8,128)(2,1)}, u32[]{:S(2)}) copy-start(bf16[2,256,1024]{2,1,0:T(8,128)(2,1)} %images.1) | copy-start | bytes 3145732
  3.1 105.4 %collective-permute-start = (bf16[256,1024]{1,0:T(8,128)(2,1)}, bf16[256,1024]{1,0:T(8,128)(2,1)}, u32[]{:S(2)}, u32[]{:S(2)}) collective-permute-start(bf16[256,1024]{1,0:T(8,128)(2,1)} %get-tuple-element.86), channel_id=1, source_target_pairs={{0,1},{1,0},{2,3},{3,2},{4,5},{5,4},{6,7},{7,6},{8,9},{9,8},{10,11... | collective-permute-start | bytes 1572872 | tf_op jit(solution)/shard_map/ppermute | solution.py:1067
  6.0 87.9 %collective-permute-start.20 = (s32[2]{0:T(128)}, s32[2]{0:T(128)S(1)}, u32[]{:S(2)}, u32[]{:S(2)}) collective-permute-start(s32[2]{0:T(128)} %param.17), channel_id=1, source_target_pairs={{0,2},{2,0},{4,6},{6,4},{8,10},{10,8},{12,14},{14,12},{16,18},{18,... | collective-permute-start | bytes 32 | tf_op jit(solution)/shard_map/ppermute | solution.py:1070
  14.8 83.1 %collective-permute-start.16 = (f32[2,1024]{1,0:T(2,128)S(1)}, f32[2,1024]{1,0:T(2,128)S(1)}, u32[]{:S(2)}, u32[]{:S(2)}) collective-permute-start(f32[2,1024]{1,0:T(2,128)S(1)} %maximum_add_fusion.pre_embed), channel_id=1, source_target_pairs={{0,2},{2,0},{4,6},{6,4},{8,10},{10,8},{12,14},{14,12},{16,18},{18,... | collective-permute-start | bytes 24584 | tf_op jit(solution)/shard_map/ppermute | solution.py:1070
  80.0 154.5 %collective-permute-start.11 = (bf16[512,1024]{1,0:T(8,128)(2,1)}, bf16[512,1024]{1,0:T(8,128)(2,1)}, u32[]{:S(2)}, u32[]{:S(2)}) collective-permute-start(bf16[512,1024]{1,0:T(8,128)(2,1)} %get-tuple-element.70.source_own), channel_id=1, source_target_pairs={{0,1},{1,0},{2,3},{3,2},{4,5},{5,4},{6,7},{7,6},{8,9},{9,8},{10,11... | collective-permute-start | bytes 3145736 | tf_op jit(solution)/shard_map/ppermute | solution.py:1067
  80.1 165.2 %collective-permute-start.9 = (bf16[512,1024]{1,0:T(8,128)(2,1)}, bf16[512,1024]{1,0:T(8,128)(2,1)S(1)}, u32[]{:S(2)}, u32[]{:S(2)}) collective-permute-start(bf16[512,1024]{1,0:T(8,128)(2,1)} %get-tuple-element.46.source.source_own), channel_id=1, source_target_pairs={{0,1},{1,0},{2,3},{3,2},{4,5},{5,4},{6,7},{7,6},{8,9},{9,8},{10,11... | collective-permute-start | bytes 3145736 | tf_op jit(solution)/shard_map/ppermute | solution.py:1067
  82.0 11.9 %copy-start.17 = (s32[2]{0:T(128)S(1)}, s32[2]{0:T(128)}, u32[]{:S(2)}) copy-start(s32[2]{0:T(128)} %param.17) | copy-start | bytes 28
  94.0 3.5 collective-permute-start.21
  97.6 3.5 collective-permute-start.22
  97.9 6.0 %collective-permute-start.17 = (f32[4,1024]{1,0:T(4,128)S(1)}, f32[4,1024]{1,0:T(4,128)S(1)}, u32[]{:S(2)}, u32[]{:S(2)}) collective-permute-start(f32[4,1024]{1,0:T(4,128)S(1)} %maximum_select_fusion.12), channel_id=1, source_target_pairs={{0,4},{2,6},{4,0},{6,2},{8,12},{10,14},{12,8},{14,10},{16,20},{18,... | collective-permute-start | bytes 49160 | tf_op jit(solution)/shard_map/ppermute | solution.py:1070
  101.3 4.4 %collective-permute-start.23 = (s32[16]{0:T(128)S(1)}, s32[16]{0:T(128)S(1)}, u32[]{:S(2)}, u32[]{:S(2)}) collective-permute-start(s32[16]{0:T(128)S(1)} %broadcast_select_fusion.2), channel_id=1, source_target_pairs={{0,16},{2,18},{4,20},{6,22},{8,24},{10,26},{12,28},{14,30},{16,0},... | collective-permute-start | bytes 200 | tf_op jit(solution)/shard_map/ppermute | solution.py:1070
  103.9 4.0 %collective-permute-start.18 = (f32[8,1024]{1,0:T(8,128)S(1)}, f32[8,1024]{1,0:T(8,128)S(1)}, u32[]{:S(2)}, u32[]{:S(2)}) collective-permute-start(f32[8,1024]{1,0:T(8,128)S(1)} %maximum_select_fusion.10), channel_id=1, source_target_pairs={{0,8},{2,10},{4,12},{6,14},{8,0},{10,2},{12,4},{14,6},{16,24},{18,... | collective-permute-start | bytes 98312 | tf_op jit(solution)/shard_map/ppermute | solution.py:1070
  107.9 108.0 %collective-permute-start.19 = (f32[16,1024]{1,0:T(8,128)S(1)}, f32[16,1024]{1,0:T(8,128)S(1)}, u32[]{:S(2)}, u32[]{:S(2)}) collective-permute-start(f32[16,1024]{1,0:T(8,128)S(1)} %maximum_select_fusion.6), channel_id=1, source_target_pairs={{0,16},{2,18},{4,20},{6,22},{8,24},{10,26},{12,28},{14,30},{16,0},... | collective-permute-start | bytes 196616 | tf_op jit(solution)/shard_map/ppermute | solution.py:1070
  166.9 15.1 %copy-start.16 = (f32[512,5]{1,0:T(8,128)S(1)}, f32[512,5]{1,0:T(8,128)}, u32[]{:S(2)}) copy-start(f32[512,5]{1,0:T(8,128)} %get-tuple-element.67) | copy-start | bytes 30724
  166.9 15.2 %copy-start.15 = (f32[512,4]{1,0:T(8,128)S(1)}, f32[512,4]{1,0:T(8,128)}, u32[]{:S(2)}) copy-start(f32[512,4]{1,0:T(8,128)} %get-tuple-element.68) | copy-start | bytes 24580
  182.4 10.7 %collective-permute-start.3 = (f32[11,256]{1,0:T(8,128)S(1)}, f32[11,256]{1,0:T(8,128)S(1)}, u32[]{:S(2)}, u32[]{:S(2)}) collective-permute-start(f32[11,256]{1,0:T(8,128)S(1)} %bitcast.84), channel_id=1, source_target_pairs={{0,1},{1,0},{2,3},{3,2},{4,5},{5,4},{6,7},{7,6},{8,9},{9,8},{10,11... | collective-permute-start | bytes 33800 | tf_op jit(solution)/shard_map/ppermute | solution.py:1067
  192.1 8.9 %copy-start.13 = (bf16[512,1024]{1,0:T(8,128)(2,1)S(1)}, bf16[512,1024]{1,0:T(8,128)(2,1)}, u32[]{:S(2)}) copy-start(bf16[512,1024]{1,0:T(8,128)(2,1)} %get-tuple-element.57) | copy-start | bytes 3145732
  193.1 1.2 collective-permute-start.12
  193.1 2.4 collective-permute-start.4
  194.3 3.7 collective-permute-start.13
  195.6 3.8 %collective-permute-start.5 = (f32[11,256]{1,0:T(8,128)S(1)}, f32[11,256]{1,0:T(8,128)S(1)}, u32[]{:S(2)}, u32[]{:S(2)}) collective-permute-start(f32[11,256]{1,0:T(8,128)S(1)} %add.60), channel_id=1, source_target_pairs={{0,4},{2,6},{4,0},{6,2},{8,12},{10,14},{12,8},{14,10},{16,20},{18,... | collective-permute-start | bytes 33800 | tf_op jit(solution)/shard_map/ppermute | solution.py:1070
  198.0 6.8 %collective-permute-start.14 = (f32[8,2,256]{2,0,1:T(8,128)S(1)}, f32[8,2,256]{2,0,1:T(8,128)S(1)}, u32[]{:S(2)}, u32[]{:S(2)}) collective-permute-start(f32[8,2,256]{2,0,1:T(8,128)S(1)} %maximum_select_fusion.11), channel_id=1, source_target_pairs={{0,8},{2,10},{4,12},{6,14},{8,0},{10,2},{12,4},{14,6},{16,24},{18,... | collective-permute-start | bytes 49160 | tf_op jit(solution)/shard_map/ppermute | solution.py:1070
  199.4 3.7 collective-permute-start.6
  201.1 27.5 %copy-start.20 = (bf16[256,1024]{1,0:T(8,128)(2,1)S(1)}, bf16[256,1024]{1,0:T(8,128)(2,1)}, u32[]{:S(2)}) copy-start(bf16[256,1024]{1,0:T(8,128)(2,1)} %get-tuple-element.65) | copy-start | bytes 1572868
  203.1 30.9 %collective-permute-start.10 = (bf16[256,1024]{1,0:T(8,128)(2,1)S(1)}, bf16[256,1024]{1,0:T(8,128)(2,1)S(1)}, u32[]{:S(2)}, u32[]{:S(2)}) collective-permute-start(bf16[256,1024]{1,0:T(8,128)(2,1)S(1)} %get-tuple-element.80), channel_id=1, source_target_pairs={{0,1},{1,0},{2,3},{3,2},{4,5},{5,4},{6,7},{7,6},{8,9},{9,8},{10,11... | collective-permute-start | bytes 1572872 | tf_op jit(solution)/shard_map/ppermute | solution.py:1067
  204.8 5.2 %collective-permute-start.7 = (f32[11,256]{1,0:T(8,128)S(1)}, f32[11,256]{1,0:T(8,128)S(1)}, u32[]{:S(2)}, u32[]{:S(2)}) collective-permute-start(f32[11,256]{1,0:T(8,128)S(1)} %add.62), channel_id=1, source_target_pairs={{0,16},{2,18},{4,20},{6,22},{8,24},{10,26},{12,28},{14,30},{16,0},... | collective-permute-start | bytes 33800 | tf_op jit(solution)/shard_map/ppermute | solution.py:1070
  210.0 4.8 %collective-permute-start.15 = (f32[16,2,256]{2,0,1:T(8,128)S(1)}, f32[16,2,256]{2,0,1:T(8,128)S(1)}, u32[]{:S(2)}, u32[]{:S(2)}) collective-permute-start(f32[16,2,256]{2,0,1:T(8,128)S(1)} %maximum_select_fusion.9), channel_id=1, source_target_pairs={{0,16},{2,18},{4,20},{6,22},{8,24},{10,26},{12,28},{14,30},{16,0},... | collective-permute-start | bytes 98312 | tf_op jit(solution)/shard_map/ppermute | solution.py:1070
  214.9 30.5 %collective-permute-start.8 = (bf16[256,1024]{1,0:T(8,128)(2,1)S(1)}, bf16[256,1024]{1,0:T(8,128)(2,1)S(1)}, u32[]{:S(2)}, u32[]{:S(2)}) collective-permute-start(bf16[256,1024]{1,0:T(8,128)(2,1)S(1)} %get-tuple-element.82), channel_id=1, source_target_pairs={{0,1},{1,0},{2,3},{3,2},{4,5},{5,4},{6,7},{7,6},{8,9},{9,8},{10,11... | collective-permute-start | bytes 1572872 | tf_op jit(solution)/shard_map/ppermute | solution.py:1067
  216.0 12.7 %collective-permute-start.24 = (f32[32,1024]{1,0:T(8,128)S(1)}, f32[32,1024]{1,0:T(8,128)S(1)}, u32[]{:S(2)}, u32[]{:S(2)}) collective-permute-start(f32[32,1024]{1,0:T(8,128)S(1)} %convolution_bitcast_fusion), channel_id=1, source_target_pairs={{0,1},{1,0},{2,3},{3,2},{4,5},{5,4},{6,7},{7,6},{8,9},{9,8},{10,11... | collective-permute-start | bytes 393224 | tf_op jit(solution)/shard_map/ppermute | solution.py:1067
  228.7 136.2 %collective-permute-start.2 = (bf16[256,1024]{1,0:T(8,128)(2,1)S(1)}, bf16[256,1024]{1,0:T(8,128)(2,1)S(1)}, u32[]{:S(2)}, u32[]{:S(2)}) collective-permute-start(bf16[256,1024]{1,0:T(8,128)(2,1)S(1)} %copy-done.20), channel_id=1, source_target_pairs={{0,1},{1,0},{2,3},{3,2},{4,5},{5,4},{6,7},{7,6},{8,9},{9,8},{10,11... | collective-permute-start | bytes 1572872 | tf_op jit(solution)/shard_map/ppermute | solution.py:1067
  234.0 144.0 %collective-permute-start.1 = (bf16[256,1024]{1,0:T(8,128)(2,1)S(1)}, bf16[256,1024]{1,0:T(8,128)(2,1)S(1)}, u32[]{:S(2)}, u32[]{:S(2)}) collective-permute-start(bf16[256,1024]{1,0:T(8,128)(2,1)S(1)} %get-tuple-element.85), channel_id=1, source_target_pairs={{0,1},{1,0},{2,3},{3,2},{4,5},{5,4},{6,7},{7,6},{8,9},{9,8},{10,11... | collective-permute-start | bytes 1572872 | tf_op jit(solution)/shard_map/ppermute | solution.py:1067
  (19 other events, 57.2 us)
